TPU v7x, 256 devices: a whole 4x4x8 slice. The times are simulated.
256 devices in a mesh: grp: 8 (over x, core), rep: 32 (over z, y).
Axes of the slice: x: 4, y: 4, z: 8, core: 2. Of those that a mesh axis runs over, the one named last changes fastest.
Arguments:
- hidden: bfloat16 [131072, 3328], P(('grp', 'rep')), may hold values from -6 to 6
- out_grad: bfloat16 [131072, 2048], P(('grp', 'rep')), may hold values from -0.09375 to 0.09375
- error_in: bfloat16 [32, 2048, 3328], P('rep', 'grp'), may hold values from -6 to 6
- initial_basis: bfloat16 [16, 3328, 64], P('grp'), may hold values from -0.109375 to 0.109375
- block_ranks: int32 [16], P('grp'), may hold values from 8 to 64, as said below
Outputs:
- new_error: float32 [32, 2048, 3328], P('rep', 'grp')
- next_basis: float32 [16, 3328, 64], P('grp')
Inputs may be any that keep to these rules, and one draw needn't show every extreme that they name: `block_ranks`: every rank is a multiple of 8; some block has rank 64 and some block rank 8.
All inputs are finite; a program needn't handle non-finite values.
Results may differ from a plain program's by a relative error of at most 0.0003.
Values may be sent and summed in bfloat16 or wider, within the bound.
No kernel may reach another device: no remote copies, remote signals or barrier semaphores. Data moves between devices by JAX's collectives and lax.ppermute only.
A program may use at most 128 MiB of HBM per device.

v0:
```python
import jax
import jax.numpy as jnp
from jax import lax
from jax.sharding import PartitionSpec as P

BLOCK = 128
RANK_MAX = 64


def orthonormal_cols(projected, active):
    gram = jnp.einsum("bck,bcl->bkl", projected, projected, precision=lax.Precision.HIGHEST)
    paired = active[:, :, None] & active[:, None, :]
    gram = jnp.where(paired, gram, jnp.eye(gram.shape[-1], dtype=gram.dtype))
    lower = jnp.linalg.cholesky(gram)
    return lax.linalg.triangular_solve(
        lower, projected, left_side=False, lower=True, transpose_a=True
    )


def project_blocks(blocks, basis):
    return jnp.einsum("bcf,bfk->bck", blocks, basis, precision=lax.Precision.HIGHEST)


def back_blocks(blocks, ortho):
    return jnp.einsum("bcf,bck->bfk", blocks, ortho, precision=lax.Precision.HIGHEST)


def per_device(hidden, out_grad, error_in, initial_basis, block_ranks):
    groups = lax.axis_size("grp")
    replicas = lax.axis_size("rep")
    shard_width = out_grad.shape[1] // groups
    gradient = lax.psum_scatter(
        lax.dot_general(
            out_grad, hidden, (((0,), (0,)), ((), ())), preferred_element_type=jnp.float32
        ),
        "grp",
        scatter_dimension=0,
        tiled=True,
    )
    combined = gradient + error_in[0].astype(jnp.float32)
    block_count = block_ranks.shape[0]
    blocks = combined.reshape(block_count, BLOCK, combined.shape[1])
    active = jnp.arange(RANK_MAX, dtype=jnp.int32)[None, :] < block_ranks[:, None]
    basis = initial_basis.astype(jnp.float32) * active[:, None, :].astype(jnp.float32)
    ortho_list = []
    back_list = []
    for position in range(block_count):
        single = blocks[position : position + 1]
        summed_p = lax.psum(project_blocks(single, basis[position : position + 1]), "rep")
        ortho_one = orthonormal_cols(summed_p, active[position : position + 1])
        back_one = lax.psum(back_blocks(single, ortho_one), "rep")
        ortho_list.append(ortho_one)
        back_list.append(back_one)
    ortho = jnp.concatenate(ortho_list, axis=0)
    summed_back = jnp.concatenate(back_list, axis=0)
    next_basis = summed_back / replicas
    approx = jnp.einsum("bck,bfk->bcf", ortho, next_basis, precision=lax.Precision.HIGHEST)
    new_error = (blocks - approx).reshape(1, shard_width, combined.shape[1])
    return (new_error, next_basis)


def solution(mesh):
    return jax.shard_map(
        per_device,
        mesh=mesh,
        in_specs=(
            P(("grp", "rep"), None),
            P(("grp", "rep"), None),
            P("rep", "grp", None),
            P("grp", None, None),
            P("grp"),
        ),
        out_specs=(P("rep", "grp", None), P("grp", None, None)),
        check_vma=False,
    )
```

profile of v0, /device:TPU:2, one launch (start us, length us, event | category | flops | bytes accessed | tf_op | source)
XLA Modules:
  0.0 518.9 jit_solution(12193441678212685280)
XLA Ops:
  7.2 0.0 copy-start
  7.2 0.0 reduce-scatter.2.cloned.1.call-start
  7.2 1.9 copy-done
  9.1 14.6 %fusion.31 = f32[2048,3328]{1,0:T(8,128)} fusion(bf16[512,2048]{1,0:T(8,128)(2,1)} %param.9, bf16[512,3328]{1,0:T(8,128)(2,1)S(1)} %copy-done), kind=kOutput, calls=%fused_computation.51 | convolution fusion | flops 6979321856 | bytes 32768000 | tf_op jit(solution)/shard_map/dot_general | solution.py:33
  23.7 0.0 copy-start.6
  23.7 0.0 reduce-scatter.2.cloned.1.call-update
  23.7 0.0 all-reduce.5.cloned.1.call-start
  23.8 0.6 copy-done.6
  24.4 0.1 iota_compare_fusion.3
  24.4 2.5 convert_multiply_fusion
  27.0 141.3 %reduce-scatter.2.cloned.1.call-done = f32[256,3328]{1,0:T(8,128)} async-done(((f32[2048,3328]{1,0:T(8,128)}), f32[256,3328]{1,0:T(8,128)}) %reduce-scatter.2.cloned.1.call-update) | async-done | bytes 3407888 | tf_op jit(solution)/shard_map/reduce_scatter | solution.py:32
  168.2 0.0 copy-start.3
  168.2 2.9 convert_add_fusion
  171.1 0.1 copy-done.3
  171.2 0.0 copy-start.1
  171.2 2.5 fusion.6
  173.7 0.0 copy-done.1
  173.7 2.5 fusion.9
  176.2 0.0 all-reduce.5.cloned.1.call-update
  176.2 0.2 all-reduce.7.cloned.1.call-start
  176.4 141.1 %all-reduce.5.cloned.1.call-done = (f32[1,128,64]{1,2,0:T(8,128)}, f32[1,128,64]{1,2,0:T(8,128)}) async-done(((f32[1,128,64]{1,2,0:T(8,128)}, f32[1,128,64]{1,2,0:T(8,128)}), (f32[1,128,64]{1,2,0:T(8,128)}, f32[1,128,64]{1,2,0:T(8,128)})) %all-reduce.5.cloned.1.call-update) | async-done | bytes 65552 | tf_op jit(solution)/shard_map/psum | solution.py:49
  317.6 0.0 copy-start.5
  317.6 1.0 convolution_select_fusion.1
  318.6 0.1 copy.8
  318.7 5.8 %custom-call.8 = f32[1,64,64]{2,1,0:T(8,128)S(1)} custom-call(f32[1,64,64]{2,1,0:T(8,128)S(1)} %fusion.20), custom_call_target="Cholesky" | custom-call | tf_op jit(solution)/shard_map/jit(cholesky)/cholesky | solution.py:14
  324.6 0.6 compare_reduce_fusion.1
  325.2 0.7 fusion.15
  325.9 4.9 custom-call.9
  330.8 1.0 fusion.25
  331.8 3.4 convolution_bitcast_fusion.1
  335.2 0.0 copy-done.5
  335.2 0.2 convolution_select_fusion
  335.4 0.1 copy.10
  335.5 0.6 fusion.19
  336.1 6.6 %custom-call.10 = f32[1,64,64]{2,1,0:T(8,128)S(1)} custom-call(f32[1,64,64]{2,1,0:T(8,128)} %fusion.19), custom_call_target="Cholesky" | custom-call | tf_op jit(solution)/shard_map/jit(cholesky)/cholesky | solution.py:14
  342.7 0.6 compare_reduce_fusion
  343.4 1.2 fusion.16
  344.5 5.7 %custom-call.11 = f32[1,1,64,64]{2,3,1,0:T(8,128)S(1)} custom-call(f32[1,1,64,64]{3,2,1,0:T(8,128)} %fusion.16), custom_call_target="InvertDiagBlocksLowerTriangular" | custom-call | tf_op jit(solution)/shard_map/triangular_solve/custom-call.0 | solution.py:15
  350.2 0.3 fusion.21
  350.5 3.4 convolution_bitcast_fusion
  353.9 0.0 all-reduce.7.cloned.1.call-update
  353.9 151.3 %all-reduce.7.cloned.1.call-done = (f32[1,3328,64]{1,2,0:T(8,128)}, f32[1,3328,64]{1,2,0:T(8,128)}) async-done(((f32[1,3328,64]{1,2,0:T(8,128)}, f32[1,3328,64]{1,2,0:T(8,128)}), (f32[1,3328,64]{1,2,0:T(8,128)}, f32[1,3328,64]{1,2,0:T(8,128)})) %all-reduce.7.cloned.1.call-update) | async-done | bytes 1703952 | tf_op jit(solution)/shard_map/psum | solution.py:51
  505.2 0.0 copy-start.2
  505.2 1.7 maximum_multiply_fusion
  506.9 0.0 copy-start.4
  506.9 0.8 copy-done.2
  507.7 4.7 convolution_subtract_fusion
  512.4 0.0 copy-done.4
  (4 shorter events, 0.1 us)
Async XLA Ops:
  7.2 2.0 copy-start
  7.2 161.1 %reduce-scatter.2.cloned.1.call-start = ((), (), s32[]{:S(2)}) async-start(), calls=%async_computation.1 | async-start | bytes 30670848 | tf_op jit(solution)/shard_map/reduce_scatter | solution.py:32
  23.7 0.7 copy-start.6
  23.7 293.8 %all-reduce.5.cloned.1.call-start = ((), (), s32[]{:S(2)}) async-start(), calls=%async_computation.2 | async-start | bytes 131072 | tf_op jit(solution)/shard_map/psum | solution.py:49
  168.2 3.0 copy-start.3
  171.2 2.5 copy-start.1
  176.2 329.0 %all-reduce.7.cloned.1.call-start = ((), (), s32[]{:S(2)}) async-start(), calls=%async_computation.3 | async-start | bytes 3407872 | tf_op jit(solution)/shard_map/psum | solution.py:51
  317.6 17.6 %copy-start.5 = (f32[1,128,64]{1,2,0:T(8,128)S(1)}, f32[1,128,64]{1,2,0:T(8,128)}, u32[]{:S(2)}) copy-start(f32[1,128,64]{1,2,0:T(8,128)} %get-tuple-element.4) | copy-start | bytes 98308
  505.2 2.5 copy-start.2
  506.9 5.5 %copy-start.4 = (f32[2,3328,64]{1,2,0:T(8,128)}, f32[2,3328,64]{1,2,0:T(8,128)S(1)}, u32[]{:S(2)}) copy-start(f32[2,3328,64]{1,2,0:T(8,128)S(1)} %maximum_multiply_fusion) | copy-start | bytes 5111812
Sparse Core Ops, SparseCore 0:
  23.9 144.3 reduce-scatter.1
  176.3 141.1 all-reduce.4
  354.0 151.1 all-reduce.6
where the time goes:
time: 520 us; the launch traced here: 519 us
  waiting for transfers between devices  434 us (83%)
  other arithmetic  34 us (7%)
  matrix products  33.6 us (6%)
  between operations  13.8 us (3%)
    psum x1, waiting for transfers between devices, per_device(): back_one = lax.psum(back_blocks(single, ortho_one), 'rep')  151 us
    reduce_scatter x1, waiting for transfers between devices, per_device(): lax.psum_scatter(lax.dot_general(out_grad, hidden, (((0,), (0,)), ((), ()...  141 us
    psum x1, waiting for transfers between devices, per_device(): lax.psum(project_blocks(single, basis[position:position + 1]), 'rep')  141 us
    dot_general x1, matrix products, per_device(): lax.dot_general(out_grad, hidden, (((0,), (0,)), ((), ())), preferred_ele...  14.6 us
    another operation x6, other arithmetic, orthonormal_cols(): lower = jnp.linalg.cholesky(gram)  13.8 us
    another operation x4, other arithmetic, orthonormal_cols(): lax.linalg.triangular_solve(lower, projected, left_side=False, lower=True...  12.4 us
  transfers between devices with their start and end apart: 3, of which 3 were waited for; matrix products, arithmetic and copies ran while one was open for 1% of the time, Pallas kernels for 0%

commit v1 on v0

v1 whole, which is shorter than its diff:
```python
import functools

import jax
import jax.numpy as jnp
from jax import lax
from jax.experimental import pallas as pl
from jax.experimental.pallas import tpu as pltpu
from jax.sharding import PartitionSpec as P

BLOCK = 128
RANK_MAX = 64
TILE = 256
PAD = 128
F32 = jnp.float32
BF16 = jnp.bfloat16
I16 = jnp.int16
PEAK = 32767.0
FINE = 64.0


def code_of(top):
    return jnp.ceil(jnp.log2(jnp.maximum(top, 1e-30)) * FINE) + 1.0


def size_of(code):
    return jnp.exp2(code * (1.0 / FINE))


def to_i16(x):
    return x.astype(jnp.int32).astype(I16)


def from_i16(x):
    return x.astype(jnp.int32).astype(F32)


def quantize(x):
    code = code_of(jnp.max(jnp.abs(x), axis=1, keepdims=True))
    return to_i16(jnp.round(x * (PEAK / size_of(code)))), code


def lanes(rows):
    return lax.broadcasted_iota(jnp.int32, (rows, PAD), 1)


def steps_of(codes):
    return size_of(from_i16(codes)) * (1.0 / PEAK)


def terms(x):
    hi = x.astype(BF16)
    rest = x - hi.astype(F32)
    return hi, rest.astype(BF16)


def dot(a, b, ca, cb):
    return lax.dot_general(a, b, (((ca,), (cb,)), ((), ())), preferred_element_type=F32)


def dot3(a, b, ca, cb):
    ah, al = terms(a)
    bh, bl = terms(b)
    return dot(ah, bh, ca, cb) + (dot(ah, bl, ca, cb) + dot(al, bh, ca, cb))


def grad_kernel(block, width, place, og, og_sib, h, h_sib, err, own, q1, q2, q3, lhs, codes):
    n = pl.program_id(0)
    tiles = width // TILE
    x, c = place[0] >> 1, place[0] & 1

    @pl.when(n == 0)
    def _():
        tok = og.shape[0]
        for d in range(4):
            owner = (x + d) & 3
            at = pl.multiple_of((owner * 2 + c) * 256 + block * BLOCK, BLOCK)
            lhs[d * BLOCK : (d + 1) * BLOCK, :tok] = og[:, pl.ds(at, BLOCK)].T
            at = pl.multiple_of(owner * 256 + block * BLOCK, BLOCK)
            lhs[d * BLOCK : (d + 1) * BLOCK, tok:] = og_sib[:, pl.ds(at, BLOCK)].T
        codes[...] = jnp.zeros_like(codes)

    tok = og.shape[0]
    total = dot(lhs[:, :tok], h[...], 1, 0) + dot(lhs[:, tok:], h_sib[...], 1, 0)
    own[...] = total[:BLOCK] + err[0].astype(F32)
    here = lanes(BLOCK) == n
    for d, out in ((1, q1), (2, q2), (3, q3)):
        part, code = quantize(total[d * BLOCK : (d + 1) * BLOCK])
        out[:, pl.ds(pl.multiple_of(n * TILE, TILE), TILE)] = part
        codes[d - 1] = jnp.where(here, code, codes[d - 1])

        @pl.when(n == tiles - 1)
        def _():
            out[:, width:] = to_i16(codes[d - 1])


def grad_chunk(place, og, og_sib, h, h_sib, err, block, first, width):
    tok, rows = og.shape
    full = lambda n, p: (0, 0)
    shape = jax.ShapeDtypeStruct((BLOCK, width + PAD), I16)
    return pl.pallas_call(
        functools.partial(grad_kernel, block, width),
        grid_spec=pltpu.PrefetchScalarGridSpec(
            num_scalar_prefetch=1,
            grid=(width // TILE,),
            in_specs=[
                pl.BlockSpec((tok, rows), full),
                pl.BlockSpec((tok, rows // 2), full),
                pl.BlockSpec((tok, TILE), lambda n, p: (0, n + first // TILE)),
                pl.BlockSpec((tok, TILE), lambda n, p: (0, n + first // TILE)),
                pl.BlockSpec((1, BLOCK, TILE), lambda n, p: (0, block, n + first // TILE)),
            ],
            out_specs=[pl.BlockSpec((BLOCK, TILE), lambda n, p: (0, n))]
            + [pl.BlockSpec((BLOCK, width + PAD), full)] * 3,
            scratch_shapes=[
                pltpu.VMEM((4 * BLOCK, 2 * tok), BF16),
                pltpu.VMEM((3, BLOCK, PAD), F32),
            ],
        ),
        out_shape=[jax.ShapeDtypeStruct((BLOCK, width), F32), shape, shape, shape],
        compiler_params=pltpu.CompilerParams(vmem_limit_bytes=30 << 20),
        cost_estimate=pl.CostEstimate(
            flops=2 * 4 * BLOCK * 2 * tok * width,
            bytes_accessed=tok * width * 4 + tok * rows * 3 + BLOCK * width * 12,
            transcendentals=0,
        ),
        name="chip_gradient",
    )(place, og, og_sib, h, h_sib, err)


def owner_kernel(width, own, r1, r2, r3, comb, zq):
    rows = own.shape[0]
    steps = [steps_of(r[:, width:]) for r in (r1, r2, r3)]
    codes = jnp.zeros((rows, PAD), F32)
    for n in range(width // TILE):
        cols = slice(n * TILE, (n + 1) * TILE)
        total = own[:, cols]
        for r, s in zip((r1, r2, r3), steps):
            total += from_i16(r[:, cols]) * s[:, n : n + 1]
        comb[:, cols] = total
        part, code = quantize(total)
        zq[:, cols] = part
        codes = jnp.where(lanes(rows) == n, code, codes)
    zq[:, width:] = to_i16(codes)


def owner_chunk(own, r1, r2, r3, width):
    rows = 32
    spec = pl.BlockSpec((rows, width + PAD), lambda n: (n, 0))
    flat = pl.BlockSpec((rows, width), lambda n: (n, 0))
    return pl.pallas_call(
        functools.partial(owner_kernel, width),
        grid=(BLOCK // rows,),
        in_specs=[flat, spec, spec, spec],
        out_specs=[flat, spec],
        out_shape=[
            jax.ShapeDtypeStruct((BLOCK, width), F32),
            jax.ShapeDtypeStruct((BLOCK, width + PAD), I16),
        ],
        compiler_params=pltpu.CompilerParams(vmem_limit_bytes=16 << 20),
        cost_estimate=pl.CostEstimate(
            flops=BLOCK * width * 30, bytes_accessed=BLOCK * width * 16, transcendentals=0
        ),
        name="sum_chips",
    )(own, r1, r2, r3)


def pair_sum(parts):
    while len(parts) > 1:
        half = len(parts) // 2
        parts = [parts[i] + parts[i + half] for i in range(half)]
    return parts[0]


def shard_kernel(width, count, *refs):
    ins, out = refs[:-1], refs[-1]
    if len(ins) == 1:
        ins = [ins[0].at[i] for i in range(count)]
    rows = out.shape[0]
    steps = [steps_of(r[:, width:]) for r in ins]
    codes = jnp.zeros((rows, PAD), F32)
    for n in range(width // TILE):
        cols = slice(n * TILE, (n + 1) * TILE)
        total = pair_sum([from_i16(r[:, cols]) * s[:, n : n + 1] for r, s in zip(ins, steps)])
        part, code = quantize(total)
        out[:, cols] = part
        codes = jnp.where(lanes(rows) == n, code, codes)
    out[:, width:] = to_i16(codes)


def shard_sum(width, count, *ins):
    rows = ins[0].shape[-2]
    return pl.pallas_call(
        functools.partial(shard_kernel, width, count),
        out_shape=jax.ShapeDtypeStruct((rows, width + PAD), I16),
        compiler_params=pltpu.CompilerParams(vmem_limit_bytes=16 << 20),
        cost_estimate=pl.CostEstimate(
            flops=count * rows * width * 10, bytes_accessed=count * rows * width * 2, transcendentals=0
        ),
        name="sum_replicas",
    )(*ins)


def factor_kernel(widths, replicas, *refs):
    count = len(widths)
    ranks, basis = refs[0], refs[1]
    sums, combs = refs[2 : 2 + count], refs[2 + count : 2 + 2 * count]
    new_error, next_t, mean = refs[2 + 2 * count :]
    rank = ranks[0]
    at = 0
    for s, width in zip(sums, widths):
        step = steps_of(s[:, width:])
        for n in range(width // TILE):
            cols = slice(n * TILE, (n + 1) * TILE)
            mean[:, at : at + TILE] = from_i16(s[:, cols]) * step[:, n : n + 1]
            at += TILE
    active = lax.broadcasted_iota(jnp.int32, (RANK_MAX, 1), 0) < rank
    active_row = lax.broadcasted_iota(jnp.int32, (1, RANK_MAX), 1) < rank
    hi, lo = terms(mean[...])
    base = basis[...]
    proj = dot(base, hi, 1, 1) + dot(base, lo, 1, 1)
    proj = jnp.where(active, proj, 0.0)
    gram = lax.dot_general(
        proj, proj, (((1,), (1,)), ((), ())), precision=lax.Precision.HIGHEST, preferred_element_type=F32
    )
    rows = lax.broadcasted_iota(jnp.int32, (RANK_MAX, RANK_MAX), 0)
    cols = lax.broadcasted_iota(jnp.int32, (RANK_MAX, RANK_MAX), 1)
    gram = jnp.where(active & active_row, gram, (rows == cols).astype(F32))
    index = lax.broadcasted_iota(jnp.int32, (RANK_MAX, 1), 0)
    ortho = proj
    for k in range(RANK_MAX):
        top = lax.rsqrt(gram[k : k + 1, k : k + 1])
        top_g = gram[k : k + 1, :] * top
        top_o = ortho[k : k + 1, :] * top
        below = jnp.where(index > k, gram[:, k : k + 1] * top, 0.0)
        gram = gram - below * top_g
        ortho = jnp.where(index == k, top_o, ortho - below * top_o)
    oh, ol = terms(ortho)
    back = (dot(oh, hi, 1, 0) + (dot(oh, lo, 1, 0) + dot(ol, hi, 1, 0))) * (1.0 / replicas)
    next_t[...] = back
    bh, bl = terms(back)
    at = 0
    for c, width in zip(combs, widths):
        part = slice(at, at + width)
        approx = dot(oh, bh[:, part], 0, 0) + (dot(oh, bl[:, part], 0, 0) + dot(ol, bh[:, part], 0, 0))
        new_error[:, part] = c[...] - approx
        at += width


def factor_block(rank, basis_t, sums, combs, widths, replicas):
    total = sum(widths)
    vmem = pl.BlockSpec(memory_space=pltpu.VMEM)
    return pl.pallas_call(
        functools.partial(factor_kernel, widths, replicas),
        in_specs=[pl.BlockSpec(memory_space=pltpu.SMEM)] + [vmem] * (1 + 2 * len(widths)),
        out_specs=[vmem, vmem],
        out_shape=[
            jax.ShapeDtypeStruct((BLOCK, total), F32),
            jax.ShapeDtypeStruct((RANK_MAX, total), F32),
        ],
        scratch_shapes=[pltpu.VMEM((BLOCK, total), F32)],
        compiler_params=pltpu.CompilerParams(vmem_limit_bytes=30 << 20),
        cost_estimate=pl.CostEstimate(
            flops=20 * BLOCK * total * RANK_MAX, bytes_accessed=BLOCK * total * 12, transcendentals=0
        ),
        name="factor",
    )(rank, basis_t, *sums, *combs)


def per_device(hidden, out_grad, error_in, initial_basis, block_ranks):
    replicas = 32
    deep, wide = 8, 4
    chips = 4
    tok, ffw = hidden.shape
    g = lax.axis_index("grp")
    core = g & 1
    place = jnp.reshape(g, (1,)).astype(jnp.int32)

    def core_perm():
        return [(x * 2 + c, x * 2 + 1 - c) for x in range(chips) for c in range(2)]

    def x_perm(d):
        return [(x * 2 + c, ((x + d) % chips) * 2 + c) for x in range(chips) for c in range(2)]

    def y_perm(d):
        return [(z * wide + y, z * wide + (y + d) % wide) for z in range(deep) for y in range(wide)]

    z_groups = [[z * wide + y for z in range(deep)] for y in range(wide)]

    split = out_grad.reshape(tok, chips, 2, 2 * BLOCK)
    away = lax.dynamic_index_in_dim(split, 1 - core, 2, keepdims=False).reshape(tok, -1)
    og_sib = lax.ppermute(away, "grp", core_perm())
    h_sib = lax.ppermute(hidden, "grp", core_perm())

    chunks = [(0, 0, ffw), (1, 0, 7 * TILE), (1, 7 * TILE, ffw - 7 * TILE)]
    basis_t = jnp.swapaxes(initial_basis, 1, 2)
    sums, combs, widths = [[], []], [[], []], [[], []]
    for block, first, width in chunks:
        own, *parts = grad_chunk(place, out_grad, og_sib, hidden, h_sib, error_in, block, first, width)
        got = [lax.ppermute(part, "grp", x_perm(d)) for d, part in zip((1, 2, 3), parts)]
        comb, zq = owner_chunk(own, *got, width)
        zq = lax.all_to_all(
            zq.reshape(deep, BLOCK // deep, width + PAD), "rep", 0, 0, tiled=True, axis_index_groups=z_groups
        )
        yq = shard_sum(width, deep, zq)
        others = [lax.ppermute(yq, "rep", y_perm(d)) for d in (1, 2, 3)]
        aq = shard_sum(width, wide, yq, *others)
        mq = lax.all_gather(aq, "rep", axis=0, tiled=True, axis_index_groups=z_groups)
        sums[block].append(mq)
        combs[block].append(comb)
        widths[block].append(width)

    errors, bases = [], []
    for block in range(2):
        e, q = factor_block(
            block_ranks[block : block + 1], basis_t[block], sums[block], combs[block], tuple(widths[block]), replicas
        )
        errors.append(e)
        bases.append(q)
    new_error = jnp.concatenate(errors, axis=0)[None]
    next_basis = jnp.swapaxes(jnp.stack(bases), 1, 2)
    return new_error, next_basis


def solution(mesh):
    return jax.shard_map(
        per_device,
        mesh=mesh,
        in_specs=(
            P(("grp", "rep"), None),
            P(("grp", "rep"), None),
            P("rep", "grp", None),
            P("grp", None, None),
            P("grp"),
        ),
        out_specs=(P("rep", "grp", None), P("grp", None, None)),
        check_vma=False,
    )
```

time: 520 us -> 276 us (0.53)
  waiting for transfers between devices: 434 us -> 30.6 us
  blocking collectives: 0 us -> 77.9 us
  starting transfers between devices: 0.3 us -> 70.3 us
  Pallas kernels: 0 us -> 59.1 us
  matrix products: 33.6 us -> 0 us
  other arithmetic: 34 us -> 3.27 us
  local copies, waits for them, and re-layouts: 3.55 us -> 30.3 us
  between operations: 13.8 us -> 0.91 us
    psum x2 -> x0, waiting for transfers between devices: 292 us -> none  [the longest x1 151 us: per_device(): back_one = lax.psum(back_blocks(single, ortho_one), 'rep')]
    reduce_scatter x1 -> x0, waiting for transfers between devices: 141 us -> none  [per_device(): lax.psum_scatter(lax.dot_general(out_grad, hidden, (((0,), (0,)), ((), ()...]
    all_gather x0 -> x3, blocking collectives: none -> 77.9 us  [per_device(): lax.all_gather(aq, 'rep', axis=0, tiled=True, axis_index_groups=z_groups)]
    pallas_call x0 -> x14, Pallas kernels: none -> 59.1 us  [the longest x3 27.7 us: grad_chunk(): pl.pallas_call(functools.partial(grad_kernel, block, width), grid_spec=pl...]
    ppermute x0 -> x20, starting transfers between devices: none -> 48.6 us  [the longest x9 32.6 us: per_device(): lax.ppermute(part, 'grp', x_perm(d))]
    dot_general x8 -> x0, matrix products: 32.3 us -> none  [the longest x1 14.6 us: per_device(): lax.dot_general(out_grad, hidden, (((0,), (0,)), ((), ())), preferred_ele...]
    ppermute x0 -> x20, waiting for transfers between devices: none -> 30.6 us  [the longest x9 26.1 us: per_device(): lax.ppermute(part, 'grp', x_perm(d))]
    another operation x10 -> x0, other arithmetic: 26.2 us -> none  [the longest x6 13.8 us: orthonormal_cols(): lower = jnp.linalg.cholesky(gram)]
  transfers between devices with their start and end apart: 3 -> 23, of which waited for: 3 -> 7; matrix products, arithmetic and copies ran while one was open for 1% -> 5% of each run, Pallas kernels for 0% -> 15%
where the time goes in v1:
time: 276 us; the launch traced here: 272 us
  blocking collectives  77.9 us (28%)
  starting transfers between devices  70.3 us (25%)
  Pallas kernels  59.1 us (21%)
  waiting for transfers between devices  30.6 us (11%)
  local copies, waits for them, and re-layouts  30.3 us (11%)
  other arithmetic  3.27 us (1%)
    all_gather x3, blocking collectives, per_device(): lax.all_gather(aq, 'rep', axis=0, tiled=True, axis_index_groups=z_groups)  77.9 us
    ppermute x9, starting transfers between devices, per_device(): lax.ppermute(part, 'grp', x_perm(d))  32.6 us
    pallas_call x3, Pallas kernels, grad_chunk(): pl.pallas_call(functools.partial(grad_kernel, block, width), grid_spec=pl...  27.7 us
    ppermute x9, waiting for transfers between devices, per_device(): lax.ppermute(part, 'grp', x_perm(d))  26.1 us
    all_to_all x3, starting transfers between devices, per_device(): lax.all_to_all(zq.reshape(deep, BLOCK // deep, width + PAD), 'rep', 0, 0,...  21.7 us
    unnamed x41, local copies, waits for them, and re-layouts  17.9 us
    pallas_call x2, Pallas kernels, factor_block(): pl.pallas_call(functools.partial(factor_kernel, widths, replicas), in_spe...  17.5 us
    ppermute x9, starting transfers between devices, per_device(): others = [lax.ppermute(yq, 'rep', y_perm(d)) for d in (1, 2, 3)]  15.4 us
  transfers between devices with their start and end apart: 23, of which 7 were waited for; matrix products, arithmetic and copies ran while one was open for 5% of the time, Pallas kernels for 15%

profile of v1, /device:TPU:2, one launch (start us, length us, event | category | flops | bytes accessed | tf_op | source)
XLA Modules:
  0.0 272.4 jit_solution(13140125278956012766)
XLA Ops:
  0.7 3.3 %reshape.24 = bf16[512,4,2,256]{3,2,1,0:T(2,128)(2,1)S(1)} reshape(bf16[512,2048]{1,0:T(8,128)(2,1)} %og.5) | data formatting | bytes 4194304 | tf_op jit(solution)/shard_map/reshape | solution.py:289
  4.1 6.5 %dynamic-slice_reduce_fusion = bf16[512,4,256]{2,1,0:T(4,128)(2,1)S(1)} fusion(bf16[512,4,2,256]{3,2,1,0:T(2,128)(2,1)S(1)} %reshape.24, s32[]{:T(128)S(6)} %select_n.4), kind=kLoop, calls=%fused_computation.1 | loop fusion | bytes 2097156 | tf_op jit(solution)/shard_map/jit(dynamic_index_in_dim)/dynamic_slice | solution.py:290
  11.4 2.3 collective-permute-done.og_sib
  13.7 2.0 copy-done.1
  15.7 6.4 %chip_gradient.5 = (f32[128,1536]{1,0:T(8,128)S(1)}, s16[128,1664]{1,0:T(8,128)(2,1)S(1)}, s16[128,1664]{1,0:T(8,128)(2,1)S(1)}, s16[128,1664]{1,0:T(8,128)(2,1)S(1)}) custom-call(s32[1]{0:T(128)} %bitcast.2.place, bf16[512,2048]{1,0:T(8,128)(2,1)S(1)} %copy-done, bf16[512,1024]{1,0:T(8,128)(2,1)S(1)} %collective-permute-done.og_sib, ...), custom_call_target="tpu_custom_call" | custom-call | flops 1610612736 | bytes 8650752 | tf_op jit(solution)/shard_map/chip_gradient/pallas_call | solution.py:100
  22.1 1.6 collective-permute-start.14
  23.7 2.8 %collective-permute-start.15 = (s16[128,1664]{1,0:T(8,128)(2,1)S(1)}, s16[128,1664]{1,0:T(8,128)(2,1)S(1)}, u32[]{:S(2)}, u32[]{:S(2)}) collective-permute-start(s16[128,1664]{1,0:T(8,128)(2,1)S(1)} %get-tuple-element.38), channel_id=1, source_target_pairs={{0,128},{32,160},{64,192},{96,224},{128,0},{160,32},{192,64},{224,... | collective-permute-start | bytes 1277960 | tf_op jit(solution)/shard_map/ppermute | solution.py:299
  26.9 8.2 %collective-permute-done.14.r1 = s16[128,1664]{1,0:T(8,128)(2,1)S(1)} collective-permute-done((s16[128,1664]{1,0:T(8,128)(2,1)S(1)}, s16[128,1664]{1,0:T(8,128)(2,1)S(1)}, u32[]{:S(2)}, u32[]{:S(2)}) %collective-permute-start.14) | collective-permute-done | bytes 426016 | tf_op jit(solution)/shard_map/ppermute | solution.py:299
  35.1 2.8 %collective-permute-done.15.r2 = s16[128,1664]{1,0:T(8,128)(2,1)S(1)} collective-permute-done((s16[128,1664]{1,0:T(8,128)(2,1)S(1)}, s16[128,1664]{1,0:T(8,128)(2,1)S(1)}, u32[]{:S(2)}, u32[]{:S(2)}) %collective-permute-start.15) | collective-permute-done | bytes 426016 | tf_op jit(solution)/shard_map/ppermute | solution.py:299
  37.9 8.2 %collective-permute-done.16.r3 = s16[128,1664]{1,0:T(8,128)(2,1)S(1)} collective-permute-done((s16[128,1664]{1,0:T(8,128)(2,1)S(1)}, s16[128,1664]{1,0:T(8,128)(2,1)S(1)}, u32[]{:S(2)}, u32[]{:S(2)}) %collective-permute-start.16) | collective-permute-done | bytes 426016 | tf_op jit(solution)/shard_map/ppermute | solution.py:299
  46.1 1.8 sum_chips.5
  49.6 8.0 %all-to-all-start.2 = ((s16[8,16,1664]{2,1,0:T(8,128)(2,1)}), s16[8,16,1664]{2,1,0:T(8,128)(2,1)}, u32[]{:S(2)}, u32[]{:S(2)}) async-start(s16[8,16,1664]{2,1,0:T(8,128)(2,1)} %bitcast.21), calls=%async_computation.2 | async-start | bytes 851968 | tf_op jit(solution)/shard_map/all_to_all | solution.py:301
  57.6 2.0 copy-done.2
  59.5 1.5 copy-done.4
  61.0 7.3 %chip_gradient.4 = (f32[128,1792]{1,0:T(8,128)S(1)}, s16[128,1920]{1,0:T(8,128)(2,1)S(1)}, s16[128,1920]{1,0:T(8,128)(2,1)S(1)}, s16[128,1920]{1,0:T(8,128)(2,1)S(1)}) custom-call(s32[1]{0:T(128)} %bitcast.2.place, bf16[512,2048]{1,0:T(8,128)(2,1)S(1)} %copy-done, bf16[512,1024]{1,0:T(8,128)(2,1)S(1)} %collective-permute-done.og_sib, ...), custom_call_target="tpu_custom_call" | custom-call | flops 1879048192 | bytes 9568256 | tf_op jit(solution)/shard_map/chip_gradient/pallas_call | solution.py:100
  69.0 1.3 collective-permute-start.8
  70.4 3.0 %collective-permute-start.9 = (s16[128,1920]{1,0:T(8,128)(2,1)S(1)}, s16[128,1920]{1,0:T(8,128)(2,1)S(1)}, u32[]{:S(2)}, u32[]{:S(2)}) collective-permute-start(s16[128,1920]{1,0:T(8,128)(2,1)S(1)} %get-tuple-element.33), channel_id=1, source_target_pairs={{0,128},{32,160},{64,192},{96,224},{128,0},{160,32},{192,64},{224,... | collective-permute-start | bytes 1474568 | tf_op jit(solution)/shard_map/ppermute | solution.py:299
  73.4 14.0 %chip_gradient.3 = (f32[128,3328]{1,0:T(8,128)S(1)}, s16[128,3456]{1,0:T(8,128)(2,1)}, s16[128,3456]{1,0:T(8,128)(2,1)}, s16[128,3456]{1,0:T(8,128)(2,1)}) custom-call(s32[1]{0:T(128)} %bitcast.2.place, bf16[512,2048]{1,0:T(8,128)(2,1)S(1)} %copy-done, bf16[512,1024]{1,0:T(8,128)(2,1)S(1)} %collective-permute-done.og_sib, bf16[512,3328]{1,0:T(8,128)(2,1)S(1)} %copy-done.2, ...), custom_call_target="tpu_custom_call" | custom-call | flops 3489660928 | bytes 15073280 | tf_op jit(solution)/shard_map/chip_gradient/pallas_call | solution.py:100
  87.4 1.2 copy-done.5
  88.6 2.4 collective-permute-start.3
  91.0 20.2 %collective-permute-start.4 = (s16[128,3456]{1,0:T(8,128)(2,1)}, s16[128,3456]{1,0:T(8,128)(2,1)S(1)}, u32[]{:S(2)}, u32[]{:S(2)}) collective-permute-start(s16[128,3456]{1,0:T(8,128)(2,1)} %get-tuple-element.27), channel_id=1, source_target_pairs={{0,192},{32,224},{64,0},{96,32},{128,64},{160,96},{192,128},{224,1... | collective-permute-start | bytes 2654216 | tf_op jit(solution)/shard_map/ppermute | solution.py:299
  111.3 2.2 sum_chips.4
  115.2 6.7 %all-to-all-start.1 = ((s16[8,16,1920]{2,1,0:T(8,128)(2,1)}), s16[8,16,1920]{2,1,0:T(8,128)(2,1)S(1)}, u32[]{:S(2)}, u32[]{:S(2)}) async-start(s16[8,16,1920]{2,1,0:T(8,128)(2,1)} %bitcast.20), calls=%async_computation.1 | async-start | bytes 983040 | tf_op jit(solution)/shard_map/all_to_all | solution.py:301
  122.8 6.9 %collective-permute-done.4.r3 = s16[128,3456]{1,0:T(8,128)(2,1)S(1)} collective-permute-done((s16[128,3456]{1,0:T(8,128)(2,1)}, s16[128,3456]{1,0:T(8,128)(2,1)S(1)}, u32[]{:S(2)}, u32[]{:S(2)}) %collective-permute-start.4) | collective-permute-done | bytes 884768 | tf_op jit(solution)/shard_map/ppermute | solution.py:299
  130.6 1.5 copy-done.6
  132.1 1.2 copy-done.12
  133.3 1.2 copy-done.14
  134.4 4.5 %sum_chips.3 = (f32[128,3328]{1,0:T(8,128)S(1)}, s16[128,3456]{1,0:T(8,128)(2,1)S(1)}) custom-call(f32[128,3328]{1,0:T(8,128)S(1)} %copy-done.6, s16[128,3456]{1,0:T(8,128)(2,1)S(1)} %collective-permute-done.2.r1, s16[128,3456]{1,0:T(8,128)(2,1)S(1)} %copy-done.12, s16[128,3456]{1,0:T(8,128)(2,1)S(1)} %copy-done.14), custom_call_target="tpu_custom_call" | custom-call | flops 12779520 | bytes 6815744 | tf_op jit(solution)/shard_map/sum_chips/pallas_call | solution.py:150
  139.9 7.1 %all-to-all-start = ((s16[8,16,3456]{2,1,0:T(8,128)(2,1)}), s16[8,16,3456]{2,1,0:T(8,128)(2,1)S(1)}, u32[]{:S(2)}, u32[]{:S(2)}) async-start(s16[8,16,3456]{2,1,0:T(8,128)(2,1)} %bitcast.17), calls=%async_computation | async-start | bytes 1769472 | tf_op jit(solution)/shard_map/all_to_all | solution.py:301
  146.9 2.0 slice_bitcast_fusion.1
  148.9 1.5 sum_replicas.10.refs_0_
  150.4 1.7 collective-permute-start.17
  152.1 2.9 %collective-permute-start.18 = (s16[16,1664]{1,0:T(8,128)(2,1)S(1)}, s16[16,1664]{1,0:T(8,128)(2,1)S(1)}, u32[]{:S(2)}, u32[]{:S(2)}) collective-permute-start(s16[16,1664]{1,0:T(8,128)(2,1)S(1)} %sum_replicas.10.refs_0_), channel_id=1, source_target_pairs={{0,2},{1,3},{2,0},{3,1},{4,6},{5,7},{6,4},{7,5},{8,10},{9,11},{10,... | collective-permute-start | bytes 159752 | tf_op jit(solution)/shard_map/ppermute | solution.py:305
  155.0 1.3 collective-permute-start.19
  157.7 1.4 collective-permute-done.19.refs_3_
  160.5 3.8 %collective-permute-start.12 = (s16[16,1920]{1,0:T(8,128)(2,1)S(1)}, s16[16,1920]{1,0:T(8,128)(2,1)S(1)}, u32[]{:S(2)}, u32[]{:S(2)}) collective-permute-start(s16[16,1920]{1,0:T(8,128)(2,1)S(1)} %sum_replicas.8.refs_0_), channel_id=1, source_target_pairs={{0,2},{1,3},{2,0},{3,1},{4,6},{5,7},{6,4},{7,5},{8,10},{9,11},{10,... | collective-permute-start | bytes 184328 | tf_op jit(solution)/shard_map/ppermute | solution.py:305
  164.4 26.7 %all_gather.11.refs_3_ = s16[128,1664]{1,0:T(8,128)(2,1)S(1)} all-gather(s16[16,1664]{1,0:T(8,128)(2,1)S(1)} %sum_replicas.11), channel_id=1, replica_groups={{0,4,8,12,16,20,24,28},{1,5,9,13,17,21,25,29},{2,6,10,14,18,22,26,30},{..., dimensions={0}, use_global_device_ids=true | all-gather | bytes 479232 | tf_op jit(solution)/shard_map/all_gather | solution.py:307
  191.6 1.3 sum_replicas.6.refs_0_
  192.9 2.1 collective-permute-start.5
  195.1 2.0 collective-permute-start.6
  197.0 1.2 collective-permute-start.7
  198.2 25.4 %all_gather.10.refs_2_ = s16[128,1920]{1,0:T(8,128)(2,1)S(1)} all-gather(s16[16,1920]{1,0:T(8,128)(2,1)S(1)} %sum_replicas.9), channel_id=1, replica_groups={{0,4,8,12,16,20,24,28},{1,5,9,13,17,21,25,29},{2,6,10,14,18,22,26,30},{..., dimensions={0}, use_global_device_ids=true | all-gather | bytes 552960 | tf_op jit(solution)/shard_map/all_gather | solution.py:307
  223.6 1.1 copy-done.16
  224.7 8.7 %factor.3 = (f32[128,3328]{1,0:T(8,128)S(1)}, f32[64,3328]{1,0:T(8,128)S(1)}) custom-call(s32[1]{0:T(128)} %get-tuple-element.49.refs_0_, bf16[64,3328]{1,0:T(8,128)(2,1)S(1)} %copy-done.7, s16[128,1920]{1,0:T(8,128)(2,1)S(1)} %all_gather.10.refs_2_, s16[128,1664]{1,0:T(8,128)(2,1)S(1)} %all_gather.11.refs_3_, f32[128,1792]{1,0:T(8,128)S(1)} %copy-done.9, ...), custom_call_target="tpu_custom_call" | custom-call | flops 545259520 | bytes 5111808 | tf_op jit(solution)/shard_map/factor/pallas_call | solution.py:252
  234.5 25.8 %all_gather.9.refs_2_ = s16[128,3456]{1,0:T(8,128)(2,1)S(1)} all-gather(s16[16,3456]{1,0:T(8,128)(2,1)S(1)} %sum_replicas.7), channel_id=1, replica_groups={{0,4,8,12,16,20,24,28},{1,5,9,13,17,21,25,29},{2,6,10,14,18,22,26,30},{..., dimensions={0}, use_global_device_ids=true | all-gather | bytes 995328 | tf_op jit(solution)/shard_map/all_gather | solution.py:307
  260.4 8.8 %factor.2 = (f32[128,3328]{1,0:T(8,128)S(1)}, f32[64,3328]{1,0:T(8,128)S(1)}) custom-call(s32[1]{0:T(128)} %get-tuple-element.48.refs_0_, bf16[64,3328]{1,0:T(8,128)(2,1)S(1)} %get-tuple-element.46.refs_1_, s16[128,3456]{1,0:T(8,128)(2,1)S(1)} %all_gather.9.refs_2_, f32[128,3328]{1,0:T(8,128)S(1)} %get-tuple-element.29.refs_3_), custom_call_target="tpu_custom_call" | custom-call | flops 545259520 | bytes 5111808 | tf_op jit(solution)/shard_map/factor/pallas_call | solution.py:252
  269.2 1.3 maximum_bitcast_fusion.1
  270.5 2.0 maximum_bitcast_fusion
  (62 shorter events, 12.7 us)
Async XLA Ops:
  0.6 13.1 %collective-permute-start.1 = (bf16[512,3328]{1,0:T(8,128)(2,1)}, bf16[512,3328]{1,0:T(8,128)(2,1)}, u32[]{:S(2)}, u32[]{:S(2)}) collective-permute-start(bf16[512,3328]{1,0:T(8,128)(2,1)} %h.5), channel_id=1, source_target_pairs={{0,32},{32,0},{64,96},{96,64},{128,160},{160,128},{192,224},{224,1... | collective-permute-start | bytes 10223624 | tf_op jit(solution)/shard_map/ppermute | solution.py:292
  4.0 9.7 %copy-start.3 = (bf16[1,256,3328]{2,1,0:T(8,128)(2,1)S(1)}, bf16[1,256,3328]{2,1,0:T(8,128)(2,1)}, u32[]{:S(2)}) copy-start(bf16[1,256,3328]{2,1,0:T(8,128)(2,1)} %err.5) | copy-start | bytes 5111812
  10.6 3.1 %copy-start = (bf16[512,2048]{1,0:T(8,128)(2,1)S(1)}, bf16[512,2048]{1,0:T(8,128)(2,1)}, u32[]{:S(2)}) copy-start(bf16[512,2048]{1,0:T(8,128)(2,1)} %og.5) | copy-start | bytes 6291460
  10.8 2.9 %collective-permute-start = (bf16[512,1024]{1,0:T(8,128)(2,1)S(1)}, bf16[512,1024]{1,0:T(8,128)(2,1)S(1)}, u32[]{:S(2)}, u32[]{:S(2)}) collective-permute-start(bf16[512,1024]{1,0:T(8,128)(2,1)S(1)} %bitcast.23), channel_id=1, source_target_pairs={{0,32},{32,0},{64,96},{96,64},{128,160},{160,128},{192,224},{224,1... | collective-permute-start | bytes 3145736 | tf_op jit(solution)/shard_map/ppermute | solution.py:291
  13.7 2.0 copy-start.1
  22.1 13.0 %collective-permute-start.14 = (s16[128,1664]{1,0:T(8,128)(2,1)S(1)}, s16[128,1664]{1,0:T(8,128)(2,1)S(1)}, u32[]{:S(2)}, u32[]{:S(2)}) collective-permute-start(s16[128,1664]{1,0:T(8,128)(2,1)S(1)} %get-tuple-element.37), channel_id=1, source_target_pairs={{0,64},{32,96},{64,128},{96,160},{128,192},{160,224},{192,0},{224,... | collective-permute-start | bytes 1277960 | tf_op jit(solution)/shard_map/ppermute | solution.py:299
  23.7 14.2 %collective-permute-start.15 = (s16[128,1664]{1,0:T(8,128)(2,1)S(1)}, s16[128,1664]{1,0:T(8,128)(2,1)S(1)}, u32[]{:S(2)}, u32[]{:S(2)}) collective-permute-start(s16[128,1664]{1,0:T(8,128)(2,1)S(1)} %get-tuple-element.38), channel_id=1, source_target_pairs={{0,128},{32,160},{64,192},{96,224},{128,0},{160,32},{192,64},{224,... | collective-permute-start | bytes 1277960 | tf_op jit(solution)/shard_map/ppermute | solution.py:299
  26.5 19.6 %collective-permute-start.16 = (s16[128,1664]{1,0:T(8,128)(2,1)S(1)}, s16[128,1664]{1,0:T(8,128)(2,1)S(1)}, u32[]{:S(2)}, u32[]{:S(2)}) collective-permute-start(s16[128,1664]{1,0:T(8,128)(2,1)S(1)} %get-tuple-element.39), channel_id=1, source_target_pairs={{0,192},{32,224},{64,0},{96,32},{128,64},{160,96},{192,128},{224,1... | collective-permute-start | bytes 1277960 | tf_op jit(solution)/shard_map/ppermute | solution.py:299
  47.9 0.9 copy-start.15
  48.8 0.8 copy-start.18
  49.6 65.6 %all-to-all-start.2 = ((s16[8,16,1664]{2,1,0:T(8,128)(2,1)}), s16[8,16,1664]{2,1,0:T(8,128)(2,1)}, u32[]{:S(2)}, u32[]{:S(2)}) async-start(s16[8,16,1664]{2,1,0:T(8,128)(2,1)} %bitcast.21), calls=%async_computation.2 | async-start | bytes 851968 | tf_op jit(solution)/shard_map/all_to_all | solution.py:301
  57.6 2.0 copy-start.2
  59.5 1.5 copy-start.4
  68.3 22.7 %collective-permute-start.10 = (s16[128,1920]{1,0:T(8,128)(2,1)S(1)}, s16[128,1920]{1,0:T(8,128)(2,1)S(1)}, u32[]{:S(2)}, u32[]{:S(2)}) collective-permute-start(s16[128,1920]{1,0:T(8,128)(2,1)S(1)} %get-tuple-element.34), channel_id=1, source_target_pairs={{0,192},{32,224},{64,0},{96,32},{128,64},{160,96},{192,128},{224,1... | collective-permute-start | bytes 1474568 | tf_op jit(solution)/shard_map/ppermute | solution.py:299
  69.0 42.2 %collective-permute-start.8 = (s16[128,1920]{1,0:T(8,128)(2,1)S(1)}, s16[128,1920]{1,0:T(8,128)(2,1)S(1)}, u32[]{:S(2)}, u32[]{:S(2)}) collective-permute-start(s16[128,1920]{1,0:T(8,128)(2,1)S(1)} %get-tuple-element.32), channel_id=1, source_target_pairs={{0,64},{32,96},{64,128},{96,160},{128,192},{160,224},{192,0},{224,... | collective-permute-start | bytes 1474568 | tf_op jit(solution)/shard_map/ppermute | solution.py:299
  70.4 40.9 %collective-permute-start.9 = (s16[128,1920]{1,0:T(8,128)(2,1)S(1)}, s16[128,1920]{1,0:T(8,128)(2,1)S(1)}, u32[]{:S(2)}, u32[]{:S(2)}) collective-permute-start(s16[128,1920]{1,0:T(8,128)(2,1)S(1)} %get-tuple-element.33), channel_id=1, source_target_pairs={{0,128},{32,160},{64,192},{96,224},{128,0},{160,32},{192,64},{224,... | collective-permute-start | bytes 1474568 | tf_op jit(solution)/shard_map/ppermute | solution.py:299
  87.4 1.2 copy-start.5
  88.6 33.2 %collective-permute-start.2 = (s16[128,3456]{1,0:T(8,128)(2,1)}, s16[128,3456]{1,0:T(8,128)(2,1)S(1)}, u32[]{:S(2)}, u32[]{:S(2)}) collective-permute-start(s16[128,3456]{1,0:T(8,128)(2,1)} %get-tuple-element.25), channel_id=1, source_target_pairs={{0,64},{32,96},{64,128},{96,160},{128,192},{160,224},{192,0},{224,... | collective-permute-start | bytes 2654216 | tf_op jit(solution)/shard_map/ppermute | solution.py:299
  88.6 33.2 %collective-permute-start.3 = (s16[128,3456]{1,0:T(8,128)(2,1)}, s16[128,3456]{1,0:T(8,128)(2,1)S(1)}, u32[]{:S(2)}, u32[]{:S(2)}) collective-permute-start(s16[128,3456]{1,0:T(8,128)(2,1)} %get-tuple-element.26), channel_id=1, source_target_pairs={{0,128},{32,160},{64,192},{96,224},{128,0},{160,32},{192,64},{224,... | collective-permute-start | bytes 2654216 | tf_op jit(solution)/shard_map/ppermute | solution.py:299
  91.0 38.7 %collective-permute-start.4 = (s16[128,3456]{1,0:T(8,128)(2,1)}, s16[128,3456]{1,0:T(8,128)(2,1)S(1)}, u32[]{:S(2)}, u32[]{:S(2)}) collective-permute-start(s16[128,3456]{1,0:T(8,128)(2,1)} %get-tuple-element.27), channel_id=1, source_target_pairs={{0,192},{32,224},{64,0},{96,32},{128,64},{160,96},{192,128},{224,1... | collective-permute-start | bytes 2654216 | tf_op jit(solution)/shard_map/ppermute | solution.py:299
  113.4 0.9 copy-start.8
  114.4 0.8 copy-start.17
  115.2 24.7 %all-to-all-start.1 = ((s16[8,16,1920]{2,1,0:T(8,128)(2,1)}), s16[8,16,1920]{2,1,0:T(8,128)(2,1)S(1)}, u32[]{:S(2)}, u32[]{:S(2)}) async-start(s16[8,16,1920]{2,1,0:T(8,128)(2,1)} %bitcast.20), calls=%async_computation.1 | async-start | bytes 983040 | tf_op jit(solution)/shard_map/all_to_all | solution.py:301
  121.8 0.9 copy-start.11
  129.7 0.9 copy-start.13
  130.6 1.5 copy-start.6
  132.1 1.2 copy-start.12
  133.3 1.2 copy-start.14
  138.9 0.9 copy-start.10
  139.9 16.5 %copy-start.19 = (s32[2]{0:T(128)S(1)}, s32[2]{0:T(128)}, u32[]{:S(2)}) copy-start(s32[2]{0:T(128)} %param.9) | copy-start | bytes 28
  139.9 51.8 %all-to-all-start = ((s16[8,16,3456]{2,1,0:T(8,128)(2,1)}), s16[8,16,3456]{2,1,0:T(8,128)(2,1)S(1)}, u32[]{:S(2)}, u32[]{:S(2)}) async-start(s16[8,16,3456]{2,1,0:T(8,128)(2,1)} %bitcast.17), calls=%async_computation | async-start | bytes 1769472 | tf_op jit(solution)/shard_map/all_to_all | solution.py:301
  150.4 6.5 %collective-permute-start.17 = (s16[16,1664]{1,0:T(8,128)(2,1)S(1)}, s16[16,1664]{1,0:T(8,128)(2,1)S(1)}, u32[]{:S(2)}, u32[]{:S(2)}) collective-permute-start(s16[16,1664]{1,0:T(8,128)(2,1)S(1)} %sum_replicas.10.refs_0_), channel_id=1, source_target_pairs={{0,1},{1,2},{2,3},{3,0},{4,5},{5,6},{6,7},{7,4},{8,9},{9,10},{10,1... | collective-permute-start | bytes 159752 | tf_op jit(solution)/shard_map/ppermute | solution.py:305
  152.1 5.6 %collective-permute-start.18 = (s16[16,1664]{1,0:T(8,128)(2,1)S(1)}, s16[16,1664]{1,0:T(8,128)(2,1)S(1)}, u32[]{:S(2)}, u32[]{:S(2)}) collective-permute-start(s16[16,1664]{1,0:T(8,128)(2,1)S(1)} %sum_replicas.10.refs_0_), channel_id=1, source_target_pairs={{0,2},{1,3},{2,0},{3,1},{4,6},{5,7},{6,4},{7,5},{8,10},{9,11},{10,... | collective-permute-start | bytes 159752 | tf_op jit(solution)/shard_map/ppermute | solution.py:305
  155.0 4.1 %collective-permute-start.19 = (s16[16,1664]{1,0:T(8,128)(2,1)S(1)}, s16[16,1664]{1,0:T(8,128)(2,1)S(1)}, u32[]{:S(2)}, u32[]{:S(2)}) collective-permute-start(s16[16,1664]{1,0:T(8,128)(2,1)S(1)} %sum_replicas.10.refs_0_), channel_id=1, source_target_pairs={{0,3},{1,0},{2,1},{3,2},{4,7},{5,4},{6,5},{7,6},{8,11},{9,8},{10,9... | collective-permute-start | bytes 159752 | tf_op jit(solution)/shard_map/ppermute | solution.py:305
  160.2 30.9 %collective-permute-start.11 = (s16[16,1920]{1,0:T(8,128)(2,1)S(1)}, s16[16,1920]{1,0:T(8,128)(2,1)S(1)}, u32[]{:S(2)}, u32[]{:S(2)}) collective-permute-start(s16[16,1920]{1,0:T(8,128)(2,1)S(1)} %sum_replicas.8.refs_0_), channel_id=1, source_target_pairs={{0,1},{1,2},{2,3},{3,0},{4,5},{5,6},{6,7},{7,4},{8,9},{9,10},{10,1... | collective-permute-start | bytes 184328 | tf_op jit(solution)/shard_map/ppermute | solution.py:305
  160.5 30.6 %collective-permute-start.12 = (s16[16,1920]{1,0:T(8,128)(2,1)S(1)}, s16[16,1920]{1,0:T(8,128)(2,1)S(1)}, u32[]{:S(2)}, u32[]{:S(2)}) collective-permute-start(s16[16,1920]{1,0:T(8,128)(2,1)S(1)} %sum_replicas.8.refs_0_), channel_id=1, source_target_pairs={{0,2},{1,3},{2,0},{3,1},{4,6},{5,7},{6,4},{7,5},{8,10},{9,11},{10,... | collective-permute-start | bytes 184328 | tf_op jit(solution)/shard_map/ppermute | solution.py:305
  164.3 26.8 %collective-permute-start.13 = (s16[16,1920]{1,0:T(8,128)(2,1)S(1)}, s16[16,1920]{1,0:T(8,128)(2,1)S(1)}, u32[]{:S(2)}, u32[]{:S(2)}) collective-permute-start(s16[16,1920]{1,0:T(8,128)(2,1)S(1)} %sum_replicas.8.refs_0_), channel_id=1, source_target_pairs={{0,3},{1,0},{2,1},{3,2},{4,7},{5,4},{6,5},{7,6},{8,11},{9,8},{10,9... | collective-permute-start | bytes 184328 | tf_op jit(solution)/shard_map/ppermute | solution.py:305
  191.6 32.0 %copy-start.7 = (bf16[64,3328]{1,0:T(8,128)(2,1)S(1)}, bf16[64,3328]{1,0:T(8,128)(2,1)}, u32[]{:S(2)}) copy-start(bf16[64,3328]{1,0:T(8,128)(2,1)} %get-tuple-element.47.refs_1_) | copy-start | bytes 1277956
  191.6 32.0 %copy-start.9 = (f32[128,1792]{1,0:T(8,128)S(1)}, f32[128,1792]{1,0:T(8,128)}, u32[]{:S(2)}) copy-start(f32[128,1792]{1,0:T(8,128)} %copy-done.8) | copy-start | bytes 2752516
  192.9 40.5 %collective-permute-start.5 = (s16[16,3456]{1,0:T(8,128)(2,1)S(1)}, s16[16,3456]{1,0:T(8,128)(2,1)S(1)}, u32[]{:S(2)}, u32[]{:S(2)}) collective-permute-start(s16[16,3456]{1,0:T(8,128)(2,1)S(1)} %sum_replicas.6.refs_0_), channel_id=1, source_target_pairs={{0,1},{1,2},{2,3},{3,0},{4,5},{5,6},{6,7},{7,4},{8,9},{9,10},{10,1... | collective-permute-start | bytes 331784 | tf_op jit(solution)/shard_map/ppermute | solution.py:305
  195.1 38.4 %collective-permute-start.6 = (s16[16,3456]{1,0:T(8,128)(2,1)S(1)}, s16[16,3456]{1,0:T(8,128)(2,1)S(1)}, u32[]{:S(2)}, u32[]{:S(2)}) collective-permute-start(s16[16,3456]{1,0:T(8,128)(2,1)S(1)} %sum_replicas.6.refs_0_), channel_id=1, source_target_pairs={{0,2},{1,3},{2,0},{3,1},{4,6},{5,7},{6,4},{7,5},{8,10},{9,11},{10,... | collective-permute-start | bytes 331784 | tf_op jit(solution)/shard_map/ppermute | solution.py:305
  197.0 36.4 %collective-permute-start.7 = (s16[16,3456]{1,0:T(8,128)(2,1)S(1)}, s16[16,3456]{1,0:T(8,128)(2,1)S(1)}, u32[]{:S(2)}, u32[]{:S(2)}) collective-permute-start(s16[16,3456]{1,0:T(8,128)(2,1)S(1)} %sum_replicas.6.refs_0_), channel_id=1, source_target_pairs={{0,3},{1,0},{2,1},{3,2},{4,7},{5,4},{6,5},{7,6},{8,11},{9,8},{10,9... | collective-permute-start | bytes 331784 | tf_op jit(solution)/shard_map/ppermute | solution.py:305
  223.6 1.1 copy-start.16

commit v2 on v0

v2 whole, which is shorter than its diff:
```python
import functools

import jax
import jax.numpy as jnp
from jax import lax
from jax.experimental import pallas as pl
from jax.experimental.pallas import tpu as pltpu
from jax.sharding import PartitionSpec as P

BLOCK = 128
RANK_MAX = 64
TILE = 256
LANE = 128
PAD = 128
F32 = jnp.float32
BF16 = jnp.bfloat16
I16 = jnp.int16
PEAK = 32767.0
SMALL = pl.CostEstimate(flops=1000, bytes_accessed=1000, transcendentals=0)
ANY = pl.BlockSpec(memory_space=pl.ANY)
VMEM = pl.BlockSpec(memory_space=pltpu.VMEM)
SMEM = pl.BlockSpec(memory_space=pltpu.SMEM)
FINE = 64.0


def code_of(top):
    return jnp.ceil(jnp.log2(jnp.maximum(top, 1e-30)) * FINE) + 1.0


def size_of(code):
    return jnp.exp2(code * (1.0 / FINE))


def to_i16(x):
    return x.astype(jnp.int32).astype(I16)


def from_i16(x):
    return x.astype(jnp.int32).astype(F32)


def quantize(x):
    code = code_of(jnp.max(jnp.abs(x), axis=0, keepdims=True))
    return to_i16(jnp.round(x * (PEAK / size_of(code)))), code


def steps_of(codes):
    return size_of(from_i16(codes)) * (1.0 / PEAK)


def terms(x):
    hi = x.astype(BF16)
    rest = x - hi.astype(F32)
    return hi, rest.astype(BF16)


def dot(a, b, ca, cb):
    return lax.dot_general(a, b, (((ca,), (cb,)), ((), ())), preferred_element_type=F32)


def dot3(a, b, ca, cb):
    ah, al = terms(a)
    bh, bl = terms(b)
    return dot(ah, bh, ca, cb) + (dot(ah, bl, ca, cb) + dot(al, bh, ca, cb))


def grad_kernel(block, width, place, og, og_sib, h, h_sib, err, *refs):
    out, lhs, codes = refs[-3:]
    half = pl.program_id(0)
    x, c = place[0] >> 1, place[0] & 1
    tok = og.shape[0]
    span = width // 2

    @pl.when(half == 0)
    def _():
        for owner in range(4):
            rows = slice(owner * BLOCK, (owner + 1) * BLOCK)
            at = pl.multiple_of(owner * 512 + c * 256 + block * BLOCK, BLOCK)
            lhs[rows, :tok] = og[:, pl.ds(at, BLOCK)].T
            at = owner * 256 + block * BLOCK
            lhs[rows, tok:] = og_sib[:, at : at + BLOCK].T
        codes[...] = jnp.zeros_like(codes)

    left, right = lhs[:, :tok], lhs[:, tok:]
    for at in range(0, span, TILE):
        size = min(TILE, span - at)
        cols = slice(at, at + size)
        total = dot(left, h[:, cols], 1, 0) + dot(right, h_sib[:, cols], 1, 0)
        memory = err[0, :, cols].astype(F32)
        for k in range(4):
            part = total[k * BLOCK : (k + 1) * BLOCK] + jnp.where(x == k, memory, 0.0)
            part, code = quantize(part)
            out[k, :, pl.ds(pl.multiple_of(half * span + at, LANE), size)] = part
            for i in range(size // LANE):
                t = half * (span // LANE) + at // LANE + i
                codes[k, pl.ds(t, 1)] = code[:, i * LANE : (i + 1) * LANE]

    @pl.when(half == 1)
    def _():
        for k in range(4):
            out[k, :, width:] = to_i16(codes[k])


def grad_chunk(place, og, og_sib, h, h_sib, err, block, after):
    tok, rows = og.shape
    width = h.shape[1]
    full = lambda n, p: (0, 0)
    return pl.pallas_call(
        functools.partial(grad_kernel, block, width),
        grid_spec=pltpu.PrefetchScalarGridSpec(
            num_scalar_prefetch=1,
            grid=(2,),
            in_specs=[
                pl.BlockSpec((tok, rows), full),
                pl.BlockSpec((tok, rows // 2), full),
                pl.BlockSpec((tok, width // 2), lambda n, p: (0, n)),
                pl.BlockSpec((tok, width // 2), lambda n, p: (0, n)),
                pl.BlockSpec((1, BLOCK, width // 2), lambda n, p: (0, block, n)),
            ]
            + [ANY] * len(after),
            out_specs=pl.BlockSpec((4, BLOCK, width + PAD), lambda n, p: (0, 0, 0)),
            scratch_shapes=[
                pltpu.VMEM((4 * BLOCK, 2 * tok), BF16),
                pltpu.VMEM((4, BLOCK, PAD), F32),
            ],
        ),
        out_shape=jax.ShapeDtypeStruct((4, BLOCK, width + PAD), I16),
        compiler_params=pltpu.CompilerParams(vmem_limit_bytes=60 << 20),
        cost_estimate=SMALL,
        name="chip_gradient",
    )(place, og, og_sib, h, h_sib, err, *after)


def pick_kernel(place, og, out):
    out[...] = og[...]


def pick(place, og):
    tok, rows = og.shape
    return pl.pallas_call(
        pick_kernel,
        grid_spec=pltpu.PrefetchScalarGridSpec(
            num_scalar_prefetch=1,
            grid=(4,),
            in_specs=[pl.BlockSpec((tok, 256), lambda n, p: (0, n * 2 + 1 - (p[0] & 1)))],
            out_specs=pl.BlockSpec((tok, 256), lambda n, p: (0, n)),
        ),
        out_shape=jax.ShapeDtypeStruct((tok, rows // 2), BF16),
        name="pick_columns",
    )(place, og)


QUARTER = BLOCK // 4


def pair_sum(parts):
    while len(parts) > 1:
        half = len(parts) // 2
        parts = [parts[i] + parts[i + half] for i in range(half)]
    return parts[0]


def owner_kernel(widths, place, *refs):
    ins, (comb, keep, s1, s2, s3, codes) = refs[:-6], refs[-6:]
    i = pl.program_id(0)
    width = sum(widths)
    at = 0
    for k, part in enumerate(widths):
        got, tail = ins[2 * k : 2 * k + 2]
        four = [got.at[j] for j in range(4)]
        steps = [steps_of(tail[j]) for j in range(4)]
        for n in range(part // LANE):
            cols = slice(n * LANE, (n + 1) * LANE)
            comb[:, at : at + LANE] = pair_sum(
                [from_i16(r[:, cols]) * s[n : n + 1] for r, s in zip(four, steps)]
            )
            at += LANE

    @pl.when(i == 3)
    def _():
        keep[...] = comb[...]

    for d, out in ((0, s1), (1, s2), (2, s3)):

        @pl.when(i == d)
        def _():
            codes[...] = jnp.zeros_like(codes)
            for n in range(width // LANE):
                cols = slice(n * LANE, (n + 1) * LANE)
                out[:, cols], codes[n : n + 1] = quantize(comb[:, cols])
            out[:, width:] = to_i16(codes[...])


def owner_chunk(y, pieces, widths, after):
    width = sum(widths)
    row = lambda n, p: ((n + 1 + p[0]) & 3, 0)
    full = lambda n, p: (0, 0)
    specs, ins = [], []
    for got, w in zip(pieces, widths):
        ins += [got, got]
        specs += [
            pl.BlockSpec((4, QUARTER, w), lambda n, p: (0, (n + 1 + p[0]) & 3, 0)),
            pl.BlockSpec((4, QUARTER, PAD), lambda n, p, w=w: (0, 0, w // PAD)),
        ]
    specs += [ANY] * len(after)
    shape = jax.ShapeDtypeStruct((QUARTER, width + PAD), I16)
    return pl.pallas_call(
        functools.partial(owner_kernel, widths),
        grid_spec=pltpu.PrefetchScalarGridSpec(
            num_scalar_prefetch=1,
            grid=(4,),
            in_specs=specs,
            out_specs=[pl.BlockSpec((QUARTER, width), row), pl.BlockSpec((QUARTER, width), full)]
            + [pl.BlockSpec((QUARTER, width + PAD), full)] * 3,
            scratch_shapes=[pltpu.VMEM((QUARTER, PAD), F32)],
        ),
        out_shape=[
            jax.ShapeDtypeStruct((BLOCK, width), F32),
            jax.ShapeDtypeStruct((QUARTER, width), F32),
            shape,
            shape,
            shape,
        ],
        compiler_params=pltpu.CompilerParams(vmem_limit_bytes=16 << 20),
        cost_estimate=SMALL,
        name="sum_chips",
    )(y, *ins, *after)


def shard_kernel(width, count, *refs):
    ins, (out, codes) = refs[:count], refs[-2:]
    steps = [None if r.dtype == F32 else steps_of(r[:, width:]) for r in ins]
    codes[...] = jnp.zeros_like(codes)
    for n in range(width // LANE):
        cols = slice(n * LANE, (n + 1) * LANE)
        total = pair_sum(
            [r[:, cols] if s is None else from_i16(r[:, cols]) * s[n : n + 1] for r, s in zip(ins, steps)]
        )
        out[:, cols], codes[n : n + 1] = quantize(total)
    out[:, width:] = to_i16(codes[...])


def shard_sum(width, ins, after):
    rows = ins[0].shape[0]
    return pl.pallas_call(
        functools.partial(shard_kernel, width, len(ins)),
        in_specs=[VMEM] * len(ins) + [ANY] * len(after),
        out_specs=VMEM,
        out_shape=jax.ShapeDtypeStruct((rows, width + PAD), I16),
        scratch_shapes=[pltpu.VMEM((rows, PAD), F32)],
        compiler_params=pltpu.CompilerParams(vmem_limit_bytes=16 << 20),
        cost_estimate=SMALL,
        name="sum_replicas",
    )(*ins, *after)


def cast_sums(sums, q, mean):
    width = mean.shape[1]
    for d, s in enumerate(sums):
        step = steps_of(s[:, width:])
        row = pl.multiple_of(((q + 4 - d) & 3) * QUARTER, QUARTER)
        for n in range(width // LANE):
            cols = slice(n * LANE, (n + 1) * LANE)
            mean[pl.ds(row, QUARTER), cols] = from_i16(s[:, cols]) * step[n : n + 1]


def factor_kernel(replicas, *refs):
    ranks, q, basis = refs[:3]
    sums, combs = (refs[3:7], refs[7:11]), refs[11:13]
    new_error, next_t, mean = refs[13:]
    row_at = lax.broadcasted_iota(jnp.int32, (8, 1), 0)
    tall = lax.broadcasted_iota(jnp.int32, (RANK_MAX, 1), 0)
    wide = lax.broadcasted_iota(jnp.int32, (1, RANK_MAX), 1)
    halves, grams, orthos, pivots = [], [], [], []
    for b in range(2):
        cast_sums(sums[b], q[0], mean)
        hi, lo = terms(mean[...])
        halves.append((hi, lo))
        rank = ranks[b]
        proj = dot(basis[b], hi, 1, 1) + dot(basis[b], lo, 1, 1)
        proj = jnp.where(tall < rank, proj, 0.0)
        gram = lax.dot_general(
            proj, proj, (((1,), (1,)), ((), ())), precision=lax.Precision.HIGHEST, preferred_element_type=F32
        )
        gram = jnp.where((tall < rank) & (wide < rank), gram, (tall == wide).astype(F32))
        grams.append([gram[8 * j : 8 * j + 8] for j in range(8)])
        orthos.append([proj[8 * j : 8 * j + 8] for j in range(8)])
        pivots.append([jnp.ones((8, 1), F32) for _ in range(8)])
    for k in range(RANK_MAX):
        at, own = divmod(k, 8)
        for gram, ortho, pivot in zip(grams, orthos, pivots):
            top = gram[at][own : own + 1, k : k + 1]
            pivot[at] = jnp.where(row_at == own, top, pivot[at])
            inverse = 1.0 / top
            top_g = gram[at][own : own + 1] * inverse
            top_o = ortho[at][own : own + 1] * inverse
            for j in range(at, 8):
                below = gram[j][:, k : k + 1]
                if j == at:
                    below = jnp.where(row_at > own, below, 0.0)
                gram[j] = gram[j] - below * top_g
                ortho[j] = ortho[j] - below * top_o
    for b in range(2):
        hi, lo = halves[b]
        scaled = [o * lax.rsqrt(p) for o, p in zip(orthos[b], pivots[b])]
        oh, ol = terms(jnp.concatenate(scaled, axis=0))
        back = (dot(oh, hi, 1, 0) + (dot(oh, lo, 1, 0) + dot(ol, hi, 1, 0))) * (1.0 / replicas)
        next_t[b] = back
        bh, bl = terms(back)
        approx = dot(oh, bh, 0, 0) + (dot(oh, bl, 0, 0) + dot(ol, bh, 0, 0))
        new_error[0, b * BLOCK : (b + 1) * BLOCK] = combs[b][...] - approx


def factor_blocks(ranks, q, basis_t, sums, combs, replicas):
    blocks, _, total = basis_t.shape
    return pl.pallas_call(
        functools.partial(factor_kernel, replicas),
        in_specs=[SMEM, SMEM] + [VMEM] * 11,
        out_specs=[VMEM, VMEM],
        out_shape=[
            jax.ShapeDtypeStruct((1, blocks * BLOCK, total), F32),
            jax.ShapeDtypeStruct((blocks, RANK_MAX, total), F32),
        ],
        scratch_shapes=[pltpu.VMEM((BLOCK, total), F32)],
        compiler_params=pltpu.CompilerParams(vmem_limit_bytes=40 << 20),
        cost_estimate=SMALL,
        name="factor",
    )(ranks, q, basis_t, *sums[0], *sums[1], *combs)


def per_device(hidden, out_grad, error_in, initial_basis, block_ranks):
    deep, wide = 8, 4
    replicas = deep * wide
    chips = 4
    g, r = lax.axis_index("grp"), lax.axis_index("rep")
    place = jnp.reshape(g, (1,)).astype(jnp.int32)
    q = jnp.reshape(jnp.where((g & 1) == 0, r & 3, r >> 3), (1,)).astype(jnp.int32)

    core_perm = [(x * 2 + c, x * 2 + 1 - c) for x in range(chips) for c in range(2)]
    x_groups = [[x * 2 + c for x in range(chips)] for c in range(2)]

    def move(array, to):
        pairs = []
        for k in range(2 * chips):
            for z in range(deep):
                for i in range(wide):
                    z2, i2 = to(k & 1, z, i)
                    pairs.append((k * replicas + z * wide + i, k * replicas + (z2 % deep) * wide + i2 % wide))
        return lax.ppermute(array, ("grp", "rep"), pairs)

    def first(d):
        return lambda c, z, i: (z + 2 * d, i) if c else (z, i + d)

    def second(d):
        return lambda c, z, i: (z, i + d) if c else (z + 2 * d, i)

    og_sib = lax.ppermute(pick(place, out_grad), "grp", core_perm)
    h_sib = lax.ppermute(hidden, "grp", core_perm)

    pieces, last = [], []
    for block in range(2):
        last.append(grad_chunk(place, out_grad, og_sib, hidden, h_sib, error_in, block, last))
        pieces.append([lax.all_to_all(last[-1], "grp", 0, 0, tiled=True, axis_index_groups=x_groups)])

    def reduce_rows(block, after):
        comb, keep, *sends = owner_chunk(q, pieces[block], (hidden.shape[1],), after)
        return comb, keep, [move(s, first(d)) for d, s in zip((1, 2, 3), sends)]

    def exchange(part):
        return [part] + [move(part, second(d)) for d in (1, 2, 3)]

    def pair(part):
        return [part, move(part, lambda c, z, i: (z ^ 1, i))]

    def gather(part):
        return [part] + [move(part, first(d)) for d in (1, 2, 3)]

    width = hidden.shape[1]
    basis_t = jnp.swapaxes(initial_basis, 1, 2)

    comb_a, keep, got = reduce_rows(0, last[-1:])
    a1 = shard_sum(width, [keep, *got], [])
    a2 = shard_sum(width, exchange(a1), [])
    comb_b, keep, got = reduce_rows(1, [a2])
    a3 = shard_sum(width, pair(a2), [keep])
    b1 = shard_sum(width, [keep, *got], [a3])
    b2 = shard_sum(width, exchange(b1), [])
    b3 = shard_sum(width, pair(b2), [])
    new_error, next_t = factor_blocks(
        block_ranks, q, basis_t, (gather(a3), gather(b3)), (comb_a, comb_b), replicas
    )
    return new_error, jnp.swapaxes(next_t, 1, 2)


def solution(mesh):
    return jax.shard_map(
        per_device,
        mesh=mesh,
        in_specs=(
            P(("grp", "rep"), None),
            P(("grp", "rep"), None),
            P("rep", "grp", None),
            P("grp", None, None),
            P("grp"),
        ),
        out_specs=(P("rep", "grp", None), P("grp", None, None)),
        check_vma=False,
    )
```

time: 520 us -> 187 us (0.36)
  waiting for transfers between devices: 434 us -> 79.7 us
  starting transfers between devices: 0.3 us -> 51.2 us
  Pallas kernels: 0 us -> 43.8 us
  other arithmetic: 34 us -> 0 us
  matrix products: 33.6 us -> 0 us
  between operations: 13.8 us -> 0.75 us
    psum x2 -> x0, waiting for transfers between devices: 292 us -> none  [the longest x1 151 us: per_device(): back_one = lax.psum(back_blocks(single, ortho_one), 'rep')]
    reduce_scatter x1 -> x0, waiting for transfers between devices: 141 us -> none  [per_device(): lax.psum_scatter(lax.dot_general(out_grad, hidden, (((0,), (0,)), ((), ()...]
    ppermute x0 -> x22, waiting for transfers between devices: none -> 46 us  [the longest x20 42 us: move(): return lax.ppermute(array, ('grp', 'rep'), pairs)]
    pallas_call x0 -> x12, Pallas kernels: none -> 43.8 us  [the longest x2 20.6 us: grad_chunk(): pl.pallas_call(functools.partial(grad_kernel, block, width), grid_spec=pl...]
    ppermute x0 -> x22, starting transfers between devices: none -> 40.1 us  [the longest x20 39.5 us: move(): return lax.ppermute(array, ('grp', 'rep'), pairs)]
    all_to_all x0 -> x2, waiting for transfers between devices: none -> 33.7 us  [per_device(): lax.all_to_all(last[-1], 'grp', 0, 0, tiled=True, axis_index_groups=x_gro...]
    dot_general x8 -> x0, matrix products: 32.3 us -> none  [the longest x1 14.6 us: per_device(): lax.dot_general(out_grad, hidden, (((0,), (0,)), ((), ())), preferred_ele...]
    another operation x10 -> x0, other arithmetic: 26.2 us -> none  [the longest x6 13.8 us: orthonormal_cols(): lower = jnp.linalg.cholesky(gram)]
  transfers between devices with their start and end apart: 3 -> 24, of which waited for: 3 -> 15; matrix products, arithmetic and copies ran while one was open for 1% -> 0% of each run, Pallas kernels for 0% -> 11%
where the time goes in v2:
time: 187 us; the launch traced here: 183 us
  waiting for transfers between devices  79.7 us (43%)
  starting transfers between devices  51.2 us (27%)
  Pallas kernels  43.8 us (23%)
  local copies, waits for them, and re-layouts  7.58 us (4%)
    ppermute x20, waiting for transfers between devices, move(): return lax.ppermute(array, ('grp', 'rep'), pairs)  42 us
    ppermute x20, starting transfers between devices, move(): return lax.ppermute(array, ('grp', 'rep'), pairs)  39.5 us
    all_to_all x2, waiting for transfers between devices, per_device(): lax.all_to_all(last[-1], 'grp', 0, 0, tiled=True, axis_index_groups=x_gro...  33.7 us
    pallas_call x2, Pallas kernels, grad_chunk(): pl.pallas_call(functools.partial(grad_kernel, block, width), grid_spec=pl...  20.6 us
    pallas_call x1, Pallas kernels, factor_blocks(): pl.pallas_call(functools.partial(factor_kernel, replicas), in_specs=[SMEM...  12.7 us
    all_to_all x2, starting transfers between devices, per_device(): lax.all_to_all(last[-1], 'grp', 0, 0, tiled=True, axis_index_groups=x_gro...  11.1 us
    unnamed x16, local copies, waits for them, and re-layouts  7.58 us
    ppermute x1, waiting for transfers between devices, per_device(): og_sib = lax.ppermute(pick(place, out_grad), 'grp', core_perm)  4.01 us
  transfers between devices with their start and end apart: 24, of which 15 were waited for; matrix products, arithmetic and copies ran while one was open for 0% of the time, Pallas kernels for 11%

profile of v2, /device:TPU:2, one launch (start us, length us, event | category | flops | bytes accessed | tf_op | source)
XLA Modules:
  0.0 183.1 jit_solution(13300042391346524355)
XLA Ops:
  0.7 3.4 %pick_columns.1 = bf16[512,1024]{1,0:T(8,128)(2,1)} custom-call(s32[1]{0:T(128)} %bitcast.2.place, bf16[512,2048]{1,0:T(8,128)(2,1)} %og.5), custom_call_target="tpu_custom_call" | custom-call | tf_op jit(solution)/shard_map/pick_columns/pallas_call | solution.py:140
  4.1 0.5 collective-permute-start
  4.6 4.0 %collective-permute-done.og_sib = bf16[512,1024]{1,0:T(8,128)(2,1)} collective-permute-done((bf16[512,1024]{1,0:T(8,128)(2,1)}, bf16[512,1024]{1,0:T(8,128)(2,1)}, u32[]{:S(2)}, u32[]{:S(2)}) %collective-permute-start) | collective-permute-done | bytes 1048608 | tf_op jit(solution)/shard_map/ppermute | solution.py:357
  8.6 1.7 copy-done.7
  10.3 10.3 %chip_gradient.2.refs_0_ = s16[4,128,3456]{2,1,0:T(8,128)(2,1)} custom-call(s32[1]{0:T(128)} %bitcast.2.place, bf16[512,2048]{1,0:T(8,128)(2,1)} %og.5, bf16[512,1024]{1,0:T(8,128)(2,1)} %collective-permute-done.og_sib, bf16[512,3328]{1,0:T(8,128)(2,1)} %h.3, bf16[512,3328]{1,0:T(8,128)(2,1)} %copy-done.7, bf16[1,256,3328]{2,1,0:T(8,128)(2,1)} %err.3), custom_call_target="tpu_custom_call" | custom-call | flops 1000 | bytes 1000 | tf_op jit(solution)/shard_map/chip_gradient/pallas_call | solution.py:108
  20.6 6.0 %all-to-all-start = ((s16[4,128,3456]{2,1,0:T(8,128)(2,1)}), s16[4,128,3456]{2,1,0:T(8,128)(2,1)S(1)}, u32[]{:S(2)}, u32[]{:S(2)}) async-start(s16[4,128,3456]{2,1,0:T(8,128)(2,1)} %chip_gradient.2.refs_0_), calls=%async_computation | async-start | bytes 7077888 | tf_op jit(solution)/shard_map/all_to_all | solution.py:363
  26.6 10.3 %chip_gradient.3.refs_2_ = s16[4,128,3456]{2,1,0:T(8,128)(2,1)} custom-call(s32[1]{0:T(128)} %bitcast.2.place, bf16[512,2048]{1,0:T(8,128)(2,1)} %og.5, bf16[512,1024]{1,0:T(8,128)(2,1)} %collective-permute-done.og_sib, bf16[512,3328]{1,0:T(8,128)(2,1)} %h.3, bf16[512,3328]{1,0:T(8,128)(2,1)} %copy-done.7, bf16[1,256,3328]{2,1,0:T(8,128)(2,1)} %err.3, ...), custom_call_target="tpu_custom_call" | custom-call | flops 1000 | bytes 1000 | tf_op jit(solution)/shard_map/chip_gradient/pallas_call | solution.py:108
  36.9 30.6 %all-to-all-done.refs_0_.refs_1_ = s16[4,128,3456]{2,1,0:T(8,128)(2,1)S(1)} async-done(((s16[4,128,3456]{2,1,0:T(8,128)(2,1)}), s16[4,128,3456]{2,1,0:T(8,128)(2,1)S(1)}, u32[]{:S(2)}, u32[]{:S(2)}) %all-to-all-start) | async-done | bytes 3538976 | tf_op jit(solution)/shard_map/all_to_all | solution.py:363
  67.5 1.8 copy-done
  69.3 5.2 %all-to-all-start.1 = ((s16[4,128,3456]{2,1,0:T(8,128)(2,1)}), s16[4,128,3456]{2,1,0:T(8,128)(2,1)S(1)}, u32[]{:S(2)}, u32[]{:S(2)}) async-start(s16[4,128,3456]{2,1,0:T(8,128)(2,1)} %chip_gradient.3.refs_2_), calls=%async_computation.1 | async-start | bytes 7077888 | tf_op jit(solution)/shard_map/all_to_all | solution.py:363
  74.4 2.0 %copy-done.1 = s16[4,128,3456]{2,1,0:T(8,128)(2,1)S(1)} copy-done((s16[4,128,3456]{2,1,0:T(8,128)(2,1)S(1)}, s16[4,128,3456]{2,1,0:T(8,128)(2,1)}, u32[]{:S(2)}) %copy-start.1) | copy-done | bytes 3538968
  76.5 2.0 %copy-done.2 = s16[4,128,3456]{2,1,0:T(8,128)(2,1)S(1)} copy-done((s16[4,128,3456]{2,1,0:T(8,128)(2,1)S(1)}, s16[4,128,3456]{2,1,0:T(8,128)(2,1)}, u32[]{:S(2)}) %copy-start.2) | copy-done | bytes 3538968
  78.5 1.8 sum_chips.2
  80.5 2.9 %collective-permute-start.3 = (s16[32,3456]{1,0:T(8,128)(2,1)S(1)}, s16[32,3456]{1,0:T(8,128)(2,1)S(1)}, u32[]{:S(2)}, u32[]{:S(2)}) collective-permute-start(s16[32,3456]{1,0:T(8,128)(2,1)S(1)} %get-tuple-element.16), channel_id=1, source_target_pairs={{0,2},{1,3},{2,0},{3,1},{4,6},{5,7},{6,4},{7,5},{8,10},{9,11},{10,... | collective-permute-start | bytes 663560 | tf_op jit(solution)/shard_map/ppermute | solution.py:349
  83.4 1.3 collective-permute-start.4
  84.7 5.1 %collective-permute-done.2.refs_1_ = s16[32,3456]{1,0:T(8,128)(2,1)S(1)} collective-permute-done((s16[32,3456]{1,0:T(8,128)(2,1)S(1)}, s16[32,3456]{1,0:T(8,128)(2,1)S(1)}, u32[]{:S(2)}, u32[]{:S(2)}) %collective-permute-start.2) | collective-permute-done | bytes 221216 | tf_op jit(solution)/shard_map/ppermute | solution.py:349
  89.8 0.9 collective-permute-done.4.refs_3_
  91.0 2.3 %collective-permute-start.5 = (s16[32,3456]{1,0:T(8,128)(2,1)S(1)}, s16[32,3456]{1,0:T(8,128)(2,1)S(1)}, u32[]{:S(2)}, u32[]{:S(2)}) collective-permute-start(s16[32,3456]{1,0:T(8,128)(2,1)S(1)} %sum_replicas.6.refs_0_), channel_id=1, source_target_pairs={{0,8},{1,9},{2,10},{3,11},{4,12},{5,13},{6,14},{7,15},{8,16},{9,17... | collective-permute-start | bytes 663560 | tf_op jit(solution)/shard_map/ppermute | solution.py:349
  93.3 5.4 %collective-permute-start.6 = (s16[32,3456]{1,0:T(8,128)(2,1)S(1)}, s16[32,3456]{1,0:T(8,128)(2,1)S(1)}, u32[]{:S(2)}, u32[]{:S(2)}) collective-permute-start(s16[32,3456]{1,0:T(8,128)(2,1)S(1)} %sum_replicas.6.refs_0_), channel_id=1, source_target_pairs={{0,16},{1,17},{2,18},{3,19},{4,20},{5,21},{6,22},{7,23},{8,24},{9,... | collective-permute-start | bytes 663560 | tf_op jit(solution)/shard_map/ppermute | solution.py:349
  98.7 2.7 %collective-permute-start.7 = (s16[32,3456]{1,0:T(8,128)(2,1)S(1)}, s16[32,3456]{1,0:T(8,128)(2,1)S(1)}, u32[]{:S(2)}, u32[]{:S(2)}) collective-permute-start(s16[32,3456]{1,0:T(8,128)(2,1)S(1)} %sum_replicas.6.refs_0_), channel_id=1, source_target_pairs={{0,24},{1,25},{2,26},{3,27},{4,28},{5,29},{6,30},{7,31},{8,0},{9,1... | collective-permute-start | bytes 663560 | tf_op jit(solution)/shard_map/ppermute | solution.py:349
  101.4 6.1 %collective-permute-done.6.refs_2_ = s16[32,3456]{1,0:T(8,128)(2,1)S(1)} collective-permute-done((s16[32,3456]{1,0:T(8,128)(2,1)S(1)}, s16[32,3456]{1,0:T(8,128)(2,1)S(1)}, u32[]{:S(2)}, u32[]{:S(2)}) %collective-permute-start.6) | collective-permute-done | bytes 221216 | tf_op jit(solution)/shard_map/ppermute | solution.py:349
  107.5 2.8 %collective-permute-done.7.refs_3_ = s16[32,3456]{1,0:T(8,128)(2,1)S(1)} collective-permute-done((s16[32,3456]{1,0:T(8,128)(2,1)S(1)}, s16[32,3456]{1,0:T(8,128)(2,1)S(1)}, u32[]{:S(2)}, u32[]{:S(2)}) %collective-permute-start.7) | collective-permute-done | bytes 221216 | tf_op jit(solution)/shard_map/ppermute | solution.py:349
  110.3 1.1 sum_replicas.7.refs_2_.refs_0_
  111.4 3.1 %all-to-all-done.1.refs_0_.refs_1_ = s16[4,128,3456]{2,1,0:T(8,128)(2,1)S(1)} async-done(((s16[4,128,3456]{2,1,0:T(8,128)(2,1)}), s16[4,128,3456]{2,1,0:T(8,128)(2,1)S(1)}, u32[]{:S(2)}, u32[]{:S(2)}) %all-to-all-start.1) | async-done | bytes 3538976 | tf_op jit(solution)/shard_map/all_to_all | solution.py:363
  114.5 1.8 sum_chips.3
  116.4 2.7 %collective-permute-start.13 = (s16[32,3456]{1,0:T(8,128)(2,1)S(1)}, s16[32,3456]{1,0:T(8,128)(2,1)S(1)}, u32[]{:S(2)}, u32[]{:S(2)}) collective-permute-start(s16[32,3456]{1,0:T(8,128)(2,1)S(1)} %get-tuple-element.20), channel_id=1, source_target_pairs={{0,2},{1,3},{2,0},{3,1},{4,6},{5,7},{6,4},{7,5},{8,10},{9,11},{10,... | collective-permute-start | bytes 663560 | tf_op jit(solution)/shard_map/ppermute | solution.py:349
  119.1 1.3 collective-permute-start.14
  120.5 1.3 sum_replicas.8.refs_4_.refs_3_
  121.8 4.1 %collective-permute-done.12.refs_1_ = s16[32,3456]{1,0:T(8,128)(2,1)S(1)} collective-permute-done((s16[32,3456]{1,0:T(8,128)(2,1)S(1)}, s16[32,3456]{1,0:T(8,128)(2,1)S(1)}, u32[]{:S(2)}, u32[]{:S(2)}) %collective-permute-start.12) | collective-permute-done | bytes 221216 | tf_op jit(solution)/shard_map/ppermute | solution.py:349
  125.9 0.9 collective-permute-done.14.refs_3_
  126.8 0.3 sum_replicas.9.refs_0_
  127.1 1.9 %collective-permute-start.15 = (s16[32,3456]{1,0:T(8,128)(2,1)S(1)}, s16[32,3456]{1,0:T(8,128)(2,1)S(1)}, u32[]{:S(2)}, u32[]{:S(2)}) collective-permute-start(s16[32,3456]{1,0:T(8,128)(2,1)S(1)} %sum_replicas.9.refs_0_), channel_id=1, source_target_pairs={{0,8},{1,9},{2,10},{3,11},{4,12},{5,13},{6,14},{7,15},{8,16},{9,17... | collective-permute-start | bytes 663560 | tf_op jit(solution)/shard_map/ppermute | solution.py:349
  129.1 5.4 %collective-permute-start.16 = (s16[32,3456]{1,0:T(8,128)(2,1)S(1)}, s16[32,3456]{1,0:T(8,128)(2,1)S(1)}, u32[]{:S(2)}, u32[]{:S(2)}) collective-permute-start(s16[32,3456]{1,0:T(8,128)(2,1)S(1)} %sum_replicas.9.refs_0_), channel_id=1, source_target_pairs={{0,16},{1,17},{2,18},{3,19},{4,20},{5,21},{6,22},{7,23},{8,24},{9,... | collective-permute-start | bytes 663560 | tf_op jit(solution)/shard_map/ppermute | solution.py:349
  134.5 2.7 %collective-permute-start.17 = (s16[32,3456]{1,0:T(8,128)(2,1)S(1)}, s16[32,3456]{1,0:T(8,128)(2,1)S(1)}, u32[]{:S(2)}, u32[]{:S(2)}) collective-permute-start(s16[32,3456]{1,0:T(8,128)(2,1)S(1)} %sum_replicas.9.refs_0_), channel_id=1, source_target_pairs={{0,24},{1,25},{2,26},{3,27},{4,28},{5,29},{6,30},{7,31},{8,0},{9,1... | collective-permute-start | bytes 663560 | tf_op jit(solution)/shard_map/ppermute | solution.py:349
  137.2 6.1 %collective-permute-done.16.refs_2_ = s16[32,3456]{1,0:T(8,128)(2,1)S(1)} collective-permute-done((s16[32,3456]{1,0:T(8,128)(2,1)S(1)}, s16[32,3456]{1,0:T(8,128)(2,1)S(1)}, u32[]{:S(2)}, u32[]{:S(2)}) %collective-permute-start.16) | collective-permute-done | bytes 221216 | tf_op jit(solution)/shard_map/ppermute | solution.py:349
  143.3 2.9 %collective-permute-done.17.refs_3_ = s16[32,3456]{1,0:T(8,128)(2,1)S(1)} collective-permute-done((s16[32,3456]{1,0:T(8,128)(2,1)S(1)}, s16[32,3456]{1,0:T(8,128)(2,1)S(1)}, u32[]{:S(2)}, u32[]{:S(2)}) %collective-permute-start.17) | collective-permute-done | bytes 221216 | tf_op jit(solution)/shard_map/ppermute | solution.py:349
  146.2 0.4 sum_replicas.10.refs_0_
  146.7 3.0 %collective-permute-start.10 = (s16[32,3456]{1,0:T(8,128)(2,1)S(1)}, s16[32,3456]{1,0:T(8,128)(2,1)S(1)}, u32[]{:S(2)}, u32[]{:S(2)}) collective-permute-start(s16[32,3456]{1,0:T(8,128)(2,1)S(1)} %sum_replicas.8.refs_4_.refs_3_), channel_id=1, source_target_pairs={{0,2},{1,3},{2,0},{3,1},{4,6},{5,7},{6,4},{7,5},{8,10},{9,11},{10,... | collective-permute-start | bytes 663560 | tf_op jit(solution)/shard_map/ppermute | solution.py:349
  149.6 1.5 collective-permute-start.11
  151.1 0.6 collective-permute-start.9
  151.6 8.0 %collective-permute-done.18.refs_1_ = s16[32,3456]{1,0:T(8,128)(2,1)S(1)} collective-permute-done((s16[32,3456]{1,0:T(8,128)(2,1)S(1)}, s16[32,3456]{1,0:T(8,128)(2,1)S(1)}, u32[]{:S(2)}, u32[]{:S(2)}) %collective-permute-start.18) | collective-permute-done | bytes 221216 | tf_op jit(solution)/shard_map/ppermute | solution.py:349
  159.9 1.7 collective-permute-start.19
  161.6 2.1 %collective-permute-start.20 = (s16[32,3456]{1,0:T(8,128)(2,1)S(1)}, s16[32,3456]{1,0:T(8,128)(2,1)S(1)}, u32[]{:S(2)}, u32[]{:S(2)}) collective-permute-start(s16[32,3456]{1,0:T(8,128)(2,1)S(1)} %sum_replicas.11.refs_7_), channel_id=1, source_target_pairs={{0,2},{1,3},{2,0},{3,1},{4,6},{5,7},{6,4},{7,5},{8,10},{9,11},{10,... | collective-permute-start | bytes 663560 | tf_op jit(solution)/shard_map/ppermute | solution.py:349
  163.7 1.7 collective-permute-start.21
  165.4 1.7 collective-permute-done.19.refs_8_
  167.2 2.8 %collective-permute-done.20.refs_9_ = s16[32,3456]{1,0:T(8,128)(2,1)S(1)} collective-permute-done((s16[32,3456]{1,0:T(8,128)(2,1)S(1)}, s16[32,3456]{1,0:T(8,128)(2,1)S(1)}, u32[]{:S(2)}, u32[]{:S(2)}) %collective-permute-start.20) | collective-permute-done | bytes 221216 | tf_op jit(solution)/shard_map/ppermute | solution.py:349
  170.0 0.4 collective-permute-done.21.refs_10_
  170.4 12.7 %factor.1 = (f32[1,256,3328]{2,1,0:T(8,128)}, f32[2,64,3328]{2,1,0:T(8,128)}) custom-call(s32[2]{0:T(128)S(1)} %copy-done.6, s32[1]{0:T(128)} %bitcast.place.refs_1_, bf16[2,64,3328]{2,1,0:T(8,128)(2,1)S(1)} %bitcast.4, s16[32,3456]{1,0:T(8,128)(2,1)S(1)} %sum_replicas.8.refs_4_.refs_3_, s16[32,3456]{1,0:T(8,128)(2,1)S(1)} %collective-permute-done.9.refs_4_, ...), custom_call_target="tpu_custom_call" | custom-call | flops 1000 | bytes 1000 | tf_op jit(solution)/shard_map/factor/pallas_call | solution.py:316
  (28 shorter events, 1.1 us)
Async XLA Ops:
  0.6 8.0 %collective-permute-start.1 = (bf16[512,3328]{1,0:T(8,128)(2,1)}, bf16[512,3328]{1,0:T(8,128)(2,1)S(1)}, u32[]{:S(2)}, u32[]{:S(2)}) collective-permute-start(bf16[512,3328]{1,0:T(8,128)(2,1)} %h.3), channel_id=1, source_target_pairs={{0,32},{32,0},{64,96},{96,64},{128,160},{160,128},{192,224},{224,1... | collective-permute-start | bytes 10223624 | tf_op jit(solution)/shard_map/ppermute | solution.py:358
  4.1 4.5 %collective-permute-start = (bf16[512,1024]{1,0:T(8,128)(2,1)}, bf16[512,1024]{1,0:T(8,128)(2,1)}, u32[]{:S(2)}, u32[]{:S(2)}) collective-permute-start(bf16[512,1024]{1,0:T(8,128)(2,1)} %pick_columns.1), channel_id=1, source_target_pairs={{0,32},{32,0},{64,96},{96,64},{128,160},{160,128},{192,224},{224,1... | collective-permute-start | bytes 3145736 | tf_op jit(solution)/shard_map/ppermute | solution.py:357
  8.6 1.8 copy-start.7
  20.6 46.9 %all-to-all-start = ((s16[4,128,3456]{2,1,0:T(8,128)(2,1)}), s16[4,128,3456]{2,1,0:T(8,128)(2,1)S(1)}, u32[]{:S(2)}, u32[]{:S(2)}) async-start(s16[4,128,3456]{2,1,0:T(8,128)(2,1)} %chip_gradient.2.refs_0_), calls=%async_computation | async-start | bytes 7077888 | tf_op jit(solution)/shard_map/all_to_all | solution.py:363
  67.5 1.8 copy-start
  69.3 45.2 %all-to-all-start.1 = ((s16[4,128,3456]{2,1,0:T(8,128)(2,1)}), s16[4,128,3456]{2,1,0:T(8,128)(2,1)S(1)}, u32[]{:S(2)}, u32[]{:S(2)}) async-start(s16[4,128,3456]{2,1,0:T(8,128)(2,1)} %chip_gradient.3.refs_2_), calls=%async_computation.1 | async-start | bytes 7077888 | tf_op jit(solution)/shard_map/all_to_all | solution.py:363
  74.4 2.0 %copy-start.1 = (s16[4,128,3456]{2,1,0:T(8,128)(2,1)S(1)}, s16[4,128,3456]{2,1,0:T(8,128)(2,1)}, u32[]{:S(2)}) copy-start(s16[4,128,3456]{2,1,0:T(8,128)(2,1)} %copy-done) | copy-start | bytes 10616836
  76.4 2.0 %copy-start.2 = (s16[4,128,3456]{2,1,0:T(8,128)(2,1)S(1)}, s16[4,128,3456]{2,1,0:T(8,128)(2,1)}, u32[]{:S(2)}) copy-start(s16[4,128,3456]{2,1,0:T(8,128)(2,1)} %chip_gradient.3.refs_2_) | copy-start | bytes 10616836
  80.2 31.2 %copy-start.3 = (f32[128,3328]{1,0:T(8,128)}, f32[128,3328]{1,0:T(8,128)S(1)}, u32[]{:S(2)}) copy-start(f32[128,3328]{1,0:T(8,128)S(1)} %get-tuple-element.22.refs_11_) | copy-start | bytes 5111812
  80.2 9.6 %collective-permute-start.2 = (s16[32,3456]{1,0:T(8,128)(2,1)S(1)}, s16[32,3456]{1,0:T(8,128)(2,1)S(1)}, u32[]{:S(2)}, u32[]{:S(2)}) collective-permute-start(s16[32,3456]{1,0:T(8,128)(2,1)S(1)} %get-tuple-element.15), channel_id=1, source_target_pairs={{0,1},{1,2},{2,3},{3,0},{4,5},{5,6},{6,7},{7,4},{8,9},{9,10},{10,1... | collective-permute-start | bytes 663560 | tf_op jit(solution)/shard_map/ppermute | solution.py:349
  80.5 9.4 %collective-permute-start.3 = (s16[32,3456]{1,0:T(8,128)(2,1)S(1)}, s16[32,3456]{1,0:T(8,128)(2,1)S(1)}, u32[]{:S(2)}, u32[]{:S(2)}) collective-permute-start(s16[32,3456]{1,0:T(8,128)(2,1)S(1)} %get-tuple-element.16), channel_id=1, source_target_pairs={{0,2},{1,3},{2,0},{3,1},{4,6},{5,7},{6,4},{7,5},{8,10},{9,11},{10,... | collective-permute-start | bytes 663560 | tf_op jit(solution)/shard_map/ppermute | solution.py:349
  83.4 7.3 %collective-permute-start.4 = (s16[32,3456]{1,0:T(8,128)(2,1)S(1)}, s16[32,3456]{1,0:T(8,128)(2,1)S(1)}, u32[]{:S(2)}, u32[]{:S(2)}) collective-permute-start(s16[32,3456]{1,0:T(8,128)(2,1)S(1)} %get-tuple-element.17), channel_id=1, source_target_pairs={{0,3},{1,0},{2,1},{3,2},{4,7},{5,4},{6,5},{7,6},{8,11},{9,8},{10,9... | collective-permute-start | bytes 663560 | tf_op jit(solution)/shard_map/ppermute | solution.py:349
  91.0 10.4 %collective-permute-start.5 = (s16[32,3456]{1,0:T(8,128)(2,1)S(1)}, s16[32,3456]{1,0:T(8,128)(2,1)S(1)}, u32[]{:S(2)}, u32[]{:S(2)}) collective-permute-start(s16[32,3456]{1,0:T(8,128)(2,1)S(1)} %sum_replicas.6.refs_0_), channel_id=1, source_target_pairs={{0,8},{1,9},{2,10},{3,11},{4,12},{5,13},{6,14},{7,15},{8,16},{9,17... | collective-permute-start | bytes 663560 | tf_op jit(solution)/shard_map/ppermute | solution.py:349
  93.3 14.2 %collective-permute-start.6 = (s16[32,3456]{1,0:T(8,128)(2,1)S(1)}, s16[32,3456]{1,0:T(8,128)(2,1)S(1)}, u32[]{:S(2)}, u32[]{:S(2)}) collective-permute-start(s16[32,3456]{1,0:T(8,128)(2,1)S(1)} %sum_replicas.6.refs_0_), channel_id=1, source_target_pairs={{0,16},{1,17},{2,18},{3,19},{4,20},{5,21},{6,22},{7,23},{8,24},{9,... | collective-permute-start | bytes 663560 | tf_op jit(solution)/shard_map/ppermute | solution.py:349
  98.7 11.6 %collective-permute-start.7 = (s16[32,3456]{1,0:T(8,128)(2,1)S(1)}, s16[32,3456]{1,0:T(8,128)(2,1)S(1)}, u32[]{:S(2)}, u32[]{:S(2)}) collective-permute-start(s16[32,3456]{1,0:T(8,128)(2,1)S(1)} %sum_replicas.6.refs_0_), channel_id=1, source_target_pairs={{0,24},{1,25},{2,26},{3,27},{4,28},{5,29},{6,30},{7,31},{8,0},{9,1... | collective-permute-start | bytes 663560 | tf_op jit(solution)/shard_map/ppermute | solution.py:349
  111.4 9.1 %collective-permute-start.8 = (s16[32,3456]{1,0:T(8,128)(2,1)}, s16[32,3456]{1,0:T(8,128)(2,1)}, u32[]{:S(2)}, u32[]{:S(2)}) collective-permute-start(s16[32,3456]{1,0:T(8,128)(2,1)} %sum_replicas.7.refs_2_.refs_0_), channel_id=1, source_target_pairs={{0,4},{1,5},{2,6},{3,7},{4,0},{5,1},{6,2},{7,3},{8,12},{9,13},{10,... | collective-permute-start | bytes 663560 | tf_op jit(solution)/shard_map/ppermute | solution.py:349
  116.3 54.1 %copy-start.4 = (f32[128,3328]{1,0:T(8,128)S(1)}, f32[128,3328]{1,0:T(8,128)}, u32[]{:S(2)}) copy-start(f32[128,3328]{1,0:T(8,128)} %copy-done.3) | copy-start | bytes 5111812
  116.3 54.1 %copy-start.5 = (bf16[2,3328,64]{1,2,0:T(8,128)(2,1)S(1)}, bf16[2,3328,64]{1,2,0:T(8,128)(2,1)}, u32[]{:S(2)}) copy-start(bf16[2,3328,64]{1,2,0:T(8,128)(2,1)} %param.8) | copy-start | bytes 2555908
  116.3 54.1 %copy-start.6 = (s32[2]{0:T(128)S(1)}, s32[2]{0:T(128)}, u32[]{:S(2)}) copy-start(s32[2]{0:T(128)} %refs_0_.1) | copy-start | bytes 28
  116.3 9.6 %collective-permute-start.12 = (s16[32,3456]{1,0:T(8,128)(2,1)S(1)}, s16[32,3456]{1,0:T(8,128)(2,1)S(1)}, u32[]{:S(2)}, u32[]{:S(2)}) collective-permute-start(s16[32,3456]{1,0:T(8,128)(2,1)S(1)} %get-tuple-element.19), channel_id=1, source_target_pairs={{0,1},{1,2},{2,3},{3,0},{4,5},{5,6},{6,7},{7,4},{8,9},{9,10},{10,1... | collective-permute-start | bytes 663560 | tf_op jit(solution)/shard_map/ppermute | solution.py:349
  116.4 9.5 %collective-permute-start.13 = (s16[32,3456]{1,0:T(8,128)(2,1)S(1)}, s16[32,3456]{1,0:T(8,128)(2,1)S(1)}, u32[]{:S(2)}, u32[]{:S(2)}) collective-permute-start(s16[32,3456]{1,0:T(8,128)(2,1)S(1)} %get-tuple-element.20), channel_id=1, source_target_pairs={{0,2},{1,3},{2,0},{3,1},{4,6},{5,7},{6,4},{7,5},{8,10},{9,11},{10,... | collective-permute-start | bytes 663560 | tf_op jit(solution)/shard_map/ppermute | solution.py:349
  119.1 7.7 %collective-permute-start.14 = (s16[32,3456]{1,0:T(8,128)(2,1)S(1)}, s16[32,3456]{1,0:T(8,128)(2,1)S(1)}, u32[]{:S(2)}, u32[]{:S(2)}) collective-permute-start(s16[32,3456]{1,0:T(8,128)(2,1)S(1)} %get-tuple-element.21), channel_id=1, source_target_pairs={{0,3},{1,0},{2,1},{3,2},{4,7},{5,4},{6,5},{7,6},{8,11},{9,8},{10,9... | collective-permute-start | bytes 663560 | tf_op jit(solution)/shard_map/ppermute | solution.py:349
  127.1 10.0 %collective-permute-start.15 = (s16[32,3456]{1,0:T(8,128)(2,1)S(1)}, s16[32,3456]{1,0:T(8,128)(2,1)S(1)}, u32[]{:S(2)}, u32[]{:S(2)}) collective-permute-start(s16[32,3456]{1,0:T(8,128)(2,1)S(1)} %sum_replicas.9.refs_0_), channel_id=1, source_target_pairs={{0,8},{1,9},{2,10},{3,11},{4,12},{5,13},{6,14},{7,15},{8,16},{9,17... | collective-permute-start | bytes 663560 | tf_op jit(solution)/shard_map/ppermute | solution.py:349
  129.1 14.2 %collective-permute-start.16 = (s16[32,3456]{1,0:T(8,128)(2,1)S(1)}, s16[32,3456]{1,0:T(8,128)(2,1)S(1)}, u32[]{:S(2)}, u32[]{:S(2)}) collective-permute-start(s16[32,3456]{1,0:T(8,128)(2,1)S(1)} %sum_replicas.9.refs_0_), channel_id=1, source_target_pairs={{0,16},{1,17},{2,18},{3,19},{4,20},{5,21},{6,22},{7,23},{8,24},{9,... | collective-permute-start | bytes 663560 | tf_op jit(solution)/shard_map/ppermute | solution.py:349
  134.5 11.7 %collective-permute-start.17 = (s16[32,3456]{1,0:T(8,128)(2,1)S(1)}, s16[32,3456]{1,0:T(8,128)(2,1)S(1)}, u32[]{:S(2)}, u32[]{:S(2)}) collective-permute-start(s16[32,3456]{1,0:T(8,128)(2,1)S(1)} %sum_replicas.9.refs_0_), channel_id=1, source_target_pairs={{0,24},{1,25},{2,26},{3,27},{4,28},{5,29},{6,30},{7,31},{8,0},{9,1... | collective-permute-start | bytes 663560 | tf_op jit(solution)/shard_map/ppermute | solution.py:349
  146.6 13.1 %collective-permute-start.18 = (s16[32,3456]{1,0:T(8,128)(2,1)S(1)}, s16[32,3456]{1,0:T(8,128)(2,1)S(1)}, u32[]{:S(2)}, u32[]{:S(2)}) collective-permute-start(s16[32,3456]{1,0:T(8,128)(2,1)S(1)} %sum_replicas.10.refs_0_), channel_id=1, source_target_pairs={{0,4},{1,5},{2,6},{3,7},{4,0},{5,1},{6,2},{7,3},{8,12},{9,13},{10,... | collective-permute-start | bytes 663560 | tf_op jit(solution)/shard_map/ppermute | solution.py:349
  146.7 17.0 %collective-permute-start.10 = (s16[32,3456]{1,0:T(8,128)(2,1)S(1)}, s16[32,3456]{1,0:T(8,128)(2,1)S(1)}, u32[]{:S(2)}, u32[]{:S(2)}) collective-permute-start(s16[32,3456]{1,0:T(8,128)(2,1)S(1)} %sum_replicas.8.refs_4_.refs_3_), channel_id=1, source_target_pairs={{0,2},{1,3},{2,0},{3,1},{4,6},{5,7},{6,4},{7,5},{8,10},{9,11},{10,... | collective-permute-start | bytes 663560 | tf_op jit(solution)/shard_map/ppermute | solution.py:349
  149.6 15.8 %collective-permute-start.11 = (s16[32,3456]{1,0:T(8,128)(2,1)S(1)}, s16[32,3456]{1,0:T(8,128)(2,1)S(1)}, u32[]{:S(2)}, u32[]{:S(2)}) collective-permute-start(s16[32,3456]{1,0:T(8,128)(2,1)S(1)} %sum_replicas.8.refs_4_.refs_3_), channel_id=1, source_target_pairs={{0,3},{1,0},{2,1},{3,2},{4,7},{5,4},{6,5},{7,6},{8,11},{9,8},{10,9... | collective-permute-start | bytes 663560 | tf_op jit(solution)/shard_map/ppermute | solution.py:349
  151.1 14.3 %collective-permute-start.9 = (s16[32,3456]{1,0:T(8,128)(2,1)S(1)}, s16[32,3456]{1,0:T(8,128)(2,1)S(1)}, u32[]{:S(2)}, u32[]{:S(2)}) collective-permute-start(s16[32,3456]{1,0:T(8,128)(2,1)S(1)} %sum_replicas.8.refs_4_.refs_3_), channel_id=1, source_target_pairs={{0,1},{1,2},{2,3},{3,0},{4,5},{5,6},{6,7},{7,4},{8,9},{9,10},{10,1... | collective-permute-start | bytes 663560 | tf_op jit(solution)/shard_map/ppermute | solution.py:349
  159.9 7.2 %collective-permute-start.19 = (s16[32,3456]{1,0:T(8,128)(2,1)S(1)}, s16[32,3456]{1,0:T(8,128)(2,1)S(1)}, u32[]{:S(2)}, u32[]{:S(2)}) collective-permute-start(s16[32,3456]{1,0:T(8,128)(2,1)S(1)} %sum_replicas.11.refs_7_), channel_id=1, source_target_pairs={{0,1},{1,2},{2,3},{3,0},{4,5},{5,6},{6,7},{7,4},{8,9},{9,10},{10,1... | collective-permute-start | bytes 663560 | tf_op jit(solution)/shard_map/ppermute | solution.py:349
  161.6 8.4 %collective-permute-start.20 = (s16[32,3456]{1,0:T(8,128)(2,1)S(1)}, s16[32,3456]{1,0:T(8,128)(2,1)S(1)}, u32[]{:S(2)}, u32[]{:S(2)}) collective-permute-start(s16[32,3456]{1,0:T(8,128)(2,1)S(1)} %sum_replicas.11.refs_7_), channel_id=1, source_target_pairs={{0,2},{1,3},{2,0},{3,1},{4,6},{5,7},{6,4},{7,5},{8,10},{9,11},{10,... | collective-permute-start | bytes 663560 | tf_op jit(solution)/shard_map/ppermute | solution.py:349
  163.7 6.7 %collective-permute-start.21 = (s16[32,3456]{1,0:T(8,128)(2,1)S(1)}, s16[32,3456]{1,0:T(8,128)(2,1)S(1)}, u32[]{:S(2)}, u32[]{:S(2)}) collective-permute-start(s16[32,3456]{1,0:T(8,128)(2,1)S(1)} %sum_replicas.11.refs_7_), channel_id=1, source_target_pairs={{0,3},{1,0},{2,1},{3,2},{4,7},{5,4},{6,5},{7,6},{8,11},{9,8},{10,9... | collective-permute-start | bytes 663560 | tf_op jit(solution)/shard_map/ppermute | solution.py:349
